TPU v7x, 128 devices: a whole 4x4x4 slice. The times are simulated.
128 devices in a mesh: section: 4 (over y), dp: 32 (over z, x, core).
Axes of the slice: x: 4, y: 4, z: 4, core: 2. Of those that a mesh axis runs over, the one named last changes fastest.
Arguments:
- old_master: float32 [49152, 4608], P(('section', 'dp')), may hold values from -0.44194174 to 0.44194174
- old_rows: int32 [49152], P(('section', 'dp')), may hold values from 0 to 49151, as said below
- gains: float32 [4, 2, 4608], P('section'), may hold values from 0.25 to 1.75
- hidden_in: bfloat16 [4, 2048, 4608], P('section', 'dp'), may hold values from -6 to 6
Outputs:
- new_master: float32 [49152, 4608], P(('section', 'dp'))
- hidden_out: bfloat16 [4, 2048, 4608], P('section', 'dp')
Inputs may be any that keep to these rules, and one draw needn't show every extreme that they name: old_rows is a permutation of 0 to 49151; global row g belongs to device g // 384 (devices numbered section-major). Of the 384 entries of each device, exactly 257 belong to the device itself and exactly 1 to each other device.
All inputs are finite; a program needn't handle non-finite values.
Results may differ from a plain program's by a relative error of at most 0.018.
Values may be sent and summed in bfloat16 or wider, within the bound.
A program may use at most 128 MiB of HBM per device.

v0:
```python
import jax
import jax.numpy as jnp
from jax import lax
from jax.sharding import PartitionSpec as P

HD = 128


epsilon = 1e-06
score_scale = 1.0 / 12.0


def swapped(shard, axis, distance):
    return lax.ppermute(shard, axis, [(i, i ^ 1 << distance) for i in range(lax.axis_size(axis))])


def passed_along(shard, axis, by):
    size = lax.axis_size(axis)
    return lax.ppermute(shard, axis, [(i, (i + by) % size) for i in range(size)])


def normed(values, gain):
    mean_square = jnp.mean(values * values, axis=-1, keepdims=True)
    return values * lax.rsqrt(mean_square + epsilon) * gain


def joined(parity_first, own_part, partner_part, axis_index):
    first = jnp.concatenate([own_part, partner_part], axis=axis_index)
    second = jnp.concatenate([partner_part, own_part], axis=axis_index)
    return jnp.where(parity_first, first, second)


def attend(queries, key_cols, value_cols):
    length = queries.shape[0]
    block = min(512, length)
    count = length // block
    starts = jnp.arange(count, dtype=jnp.int32) * block

    def one_block(start):
        query_block = lax.dynamic_slice_in_dim(queries, start, block, 0)
        scores = (
            lax.dot_general(
                query_block, key_cols, (((1,), (1,)), ((), ())), preferred_element_type=jnp.float32
            )
            * score_scale
        )
        causal = start + lax.broadcasted_iota(
            jnp.int32, (block, length), 0
        ) >= lax.broadcasted_iota(jnp.int32, (block, length), 1)
        scores = jnp.where(causal, scores, -1e30)
        row_max = jnp.max(scores, axis=-1, keepdims=True)
        exps = jnp.exp(scores - row_max)
        probabilities = (exps / jnp.sum(exps, axis=-1, keepdims=True)).astype(jnp.bfloat16)
        return jnp.dot(probabilities, value_cols, preferred_element_type=jnp.float32).astype(
            jnp.bfloat16
        )

    return lax.map(one_block, starts).reshape(length, value_cols.shape[1])


def body(old_master, old_rows, gains, hidden_in):
    n_section = lax.axis_size("section")
    n_data = lax.axis_size("dp")
    devices = n_section * n_data
    slab_rows = old_master.shape[0]
    model_width = old_master.shape[1]
    peer_rows = slab_rows // (3 * devices)
    keep_rows = slab_rows - (devices - 1) * peer_rows
    half_head = HD // 2
    self_index = lax.axis_index("section") * n_data + lax.axis_index("dp")
    owners = old_rows // slab_rows
    sorted_order = jnp.argsort(owners, stable=True)
    targets = jnp.arange(devices, dtype=jnp.int32)
    first_rows = targets * peer_rows + jnp.where(targets > self_index, keep_rows - peer_rows, 0)
    send_index = (first_rows[:, None] + jnp.arange(peer_rows, dtype=jnp.int32)[None, :]).reshape(
        devices * peer_rows
    )
    kept_index = (
        self_index * peer_rows + peer_rows + jnp.arange(keep_rows - peer_rows, dtype=jnp.int32)
    )
    send_rows = sorted_order[send_index]
    kept_rows = sorted_order[kept_index]
    moving = old_master[send_rows]
    labels = old_rows[send_rows].astype(jnp.float32)
    arrived, arrived_labels = (
        lax.all_to_all(
            moving.reshape(devices, peer_rows, model_width),
            ("section", "dp"),
            split_axis=0,
            concat_axis=0,
            tiled=True,
        ),
        lax.all_to_all(
            labels.reshape(devices, peer_rows),
            ("section", "dp"),
            split_axis=0,
            concat_axis=0,
            tiled=True,
        ),
    )
    arrived = arrived.reshape(devices * peer_rows, model_width)
    arrived_places = arrived_labels.reshape(devices * peer_rows).astype(jnp.int32) % slab_rows
    kept_places = old_rows[kept_rows] % slab_rows
    gathered_rows = jnp.concatenate([arrived, old_master[kept_rows]], axis=0)
    places = jnp.concatenate([arrived_places, kept_places], axis=0)
    master = gathered_rows[jnp.argsort(places)]
    weights = master.astype(jnp.bfloat16)
    query_rows = weights[:HD]
    pair_rows = weights[HD : 2 * HD]
    output_rows = weights[2 * HD :]
    parity_first = lax.axis_index("dp") % 2 == 0
    partner_rows = swapped(pair_rows, "dp", 0)
    key_rows = joined(parity_first, pair_rows[:half_head], partner_rows[:half_head], 0)
    value_rows = joined(parity_first, pair_rows[half_head:], partner_rows[half_head:], 0)
    project_rows = jnp.concatenate([query_rows, key_rows, value_rows], axis=0)
    gain_before = gains[0, 0]
    gain_after = gains[0, 1]
    current = hidden_in[0]
    resident = current.astype(jnp.float32)
    scaled = normed(resident, gain_before).astype(jnp.bfloat16)
    projected = lax.dot_general(
        lax.all_gather(scaled, "dp", axis=0, tiled=True),
        project_rows,
        (((1,), (1,)), ((), ())),
        preferred_element_type=jnp.float32,
    ).astype(jnp.bfloat16)
    queries = projected[:, :HD]
    key_cols = projected[:, HD : 2 * HD]
    value_cols = projected[:, 2 * HD :]
    attended = attend(queries, key_cols, value_cols)
    summed = lax.psum_scatter(
        jnp.dot(attended, output_rows, preferred_element_type=jnp.float32).astype(jnp.bfloat16),
        "dp",
        scatter_dimension=0,
        tiled=True,
    ).astype(jnp.float32)
    updated = (resident + normed(summed, gain_after)).astype(jnp.bfloat16)
    current = passed_along(updated, "section", 1)
    return (master, current[None])


def solution(mesh):
    in_specs = (
        P(("section", "dp"), None),
        P(("section", "dp")),
        P("section", None, None),
        P("section", "dp", None),
    )
    out_specs = (P(("section", "dp"), None), P("section", "dp", None))
    return jax.shard_map(body, mesh=mesh, in_specs=in_specs, out_specs=out_specs, check_vma=False)
```

profile of v0, /device:TPU:0, one launch (start us, length us, event | category | flops | bytes accessed | tf_op | source)
XLA Modules:
  0.0 338.7 jit_solution(10087789792275333070)
XLA Ops:
  7.2 1.5 slice_reduce_fusion
  10.1 2.1 fusion.20
  12.2 3.8 %sort.34 = (s32[384]{0:T(512)}, s32[384]{0:T(512)S(1)}) sort(s32[384]{0:T(512)S(1)} %add_select_fusion, s32[384]{0:T(512)S(1)} %iota.32), dimensions={0}, to_apply=%region_0.1 | sort | flops 3456 | bytes 6144 | tf_op jit(solution)/shard_map/jit(argsort)/sort | solution.py:72
  19.3 11.1 %all-to-all-start.1 = ((f32[128,1,1]{2,1,0:T(1,128)}), f32[128,1,1]{2,1,0:T(1,128)S(1)}, u32[]{:S(2)}, u32[]{:S(2)}) async-start(f32[128,1,1]{2,1,0:T(1,128)} %copy.9), calls=%async_computation.1 | async-start | bytes 131072 | tf_op jit(solution)/shard_map/all_to_all | solution.py:93
  30.5 5.6 %gather_fusion.1 = f32[128,4608]{1,0:T(8,128)S(1)} fusion(f32[384,4608]{1,0:T(8,128)} %param.6, s32[1024]{0:T(1024)S(1)} %pad_clamp_fusion.3), kind=kCustom, calls=%fused_computation.1 | custom fusion | bytes 4719104 | tf_op jit(solution)/shard_map/gather | solution.py:83
  36.1 3.8 %copy.8 = f32[128,1,4608]{2,1,0:T(1,128)} copy(f32[128,1,4608]{2,0,1:T(8,128)S(1)} %bitcast.39) | data formatting | bytes 4718592 | tf_op jit(solution)/shard_map/reshape | solution.py:87
  39.9 9.7 %all-to-all-start = ((f32[128,1,4608]{2,1,0:T(1,128)}), f32[128,1,4608]{2,1,0:T(1,128)S(1)}, u32[]{:S(2)}, u32[]{:S(2)}) async-start(f32[128,1,4608]{2,1,0:T(1,128)} %copy.8), calls=%async_computation | async-start | bytes 4718592 | tf_op jit(solution)/shard_map/all_to_all | solution.py:86
  49.9 1.9 gather_fusion.2
  51.9 9.3 %gather_fusion.3 = f32[256,4608]{1,0:T(8,128)} fusion(f32[384,4608]{1,0:T(8,128)} %param.6, s32[1024]{0:T(1024)S(1)} %pad_clamp_fusion.1), kind=kCustom, calls=%fused_computation.3 | custom fusion | bytes 9438208 | tf_op jit(solution)/shard_map/gather | solution.py:104
  61.2 1.9 gather_fusion.5
  63.2 2.5 remainder_reduce_fusion
  65.6 3.8 %sort.35 = (s32[384]{0:T(512)}, s32[384]{0:T(512)S(1)}) sort(s32[384]{0:T(512)S(1)} %pad_add_fusion, s32[384]{0:T(512)S(1)} %iota.36), dimensions={0}, to_apply=%region_1.2 | sort | flops 3456 | bytes 6144 | tf_op jit(solution)/shard_map/jit(argsort)/sort | solution.py:106
  69.4 38.7 %all-to-all-done = f32[128,1,4608]{2,1,0:T(1,128)S(1)} async-done(((f32[128,1,4608]{2,1,0:T(1,128)}), f32[128,1,4608]{2,1,0:T(1,128)S(1)}, u32[]{:S(2)}, u32[]{:S(2)}) %all-to-all-start) | async-done | bytes 2359328 | tf_op jit(solution)/shard_map/all_to_all | solution.py:86
  108.3 2.2 copy-done.1
  110.4 3.3 pad_maximum_fusion
  113.8 12.2 %gather_fusion.6 = f32[384,4608]{1,0:T(8,128)} fusion(f32[384,4608]{1,0:T(8,128)} %pad_maximum_fusion, s32[1024]{0:T(1024)S(1)} %pad_clamp_fusion), kind=kCustom, calls=%fused_computation.6 | custom fusion | bytes 14157312 | tf_op jit(solution)/shard_map/gather | solution.py:106
  126.0 3.4 convert_element_type.54
  129.3 1.6 fusion.29
  131.0 3.1 collective-permute-done
  135.4 1.8 maximum_select_fusion
  137.2 14.9 %fusion.13 = bf16[2048,384]{1,0:T(8,128)(2,1)S(1)} fusion(bf16[2048,4608]{1,0:T(8,128)(2,1)} %all-gather.2.cloned.1.call-done, bf16[128,4608]{1,0:T(8,128)(2,1)} %get-tuple-element.65, bf16[128,4608]{1,0:T(8,128)(2,1)} %get-tuple-element.64, bf16[128,4608]{1,0:T(8,128)(2,1)} %get-tuple-element.55), kind=kOutput, calls=%fused_computation.27 | convolution fusion | flops 7259160576 | bytes 23986176 | tf_op jit(solution)/shard_map/dot_general | solution.py:121
  153.3 32.4 %while.10 = (s32[]{:T(128)}, bf16[4,512,128]{2,1,0:T(8,128)(2,1)}, s32[4]{0:T(128)S(1)}, bf16[2048,128]{1,0:T(8,128)(2,1)}, bf16[2048,128]{1,0:T(8,128)(2,1)}, /...) while((s32[]{:T(128)}, bf16[4,512,128]{2,1,0:T(8,128)(2,1)}, s32[4]{0:T(128)S(1)}, ...), condition=%wide.region_6.7_spmd, body=%wide.region_3.6_spmd.sunk | while | flops 546373120 | bytes 16005807 | solution.py:58
  156.8 2.1 fusion.44
  164.9 2.1 fusion.44
  168.0 1.5 fusion.46
  173.0 2.1 fusion.44
  176.1 1.5 fusion.46
  181.1 2.1 fusion.44
  185.7 10.1 %convolution_convert_fusion = bf16[2048,4608]{1,0:T(8,128)(2,1)} fusion(bf16[2048,128]{1,0:T(8,128)(2,1)} %bitcast.12, bf16[384,4608]{1,0:T(8,128)(2,1)S(1)} %convert_element_type.54), kind=kOutput, calls=%fused_computation.19 | convolution fusion | flops 2425356288 | bytes 20578304 | tf_op jit(solution)/shard_map/dot_general | solution.py:132
  195.9 117.3 %reduce-scatter.2.cloned.1.call-done = bf16[64,4608]{1,0:T(8,128)(2,1)} async-done(((bf16[2048,4608]{1,0:T(8,128)(2,1)}), bf16[64,4608]{1,0:T(8,128)(2,1)}) %reduce-scatter.2.cloned.1.call-update) | async-done | bytes 589840 | tf_op jit(solution)/shard_map/reduce_scatter | solution.py:131
  315.8 1.5 collective-permute-start.1
  317.3 13.7 %collective-permute-done.1 = bf16[64,4608]{1,0:T(8,128)(2,1)S(1)} collective-permute-done((bf16[64,4608]{1,0:T(8,128)(2,1)S(1)}, bf16[64,4608]{1,0:T(8,128)(2,1)S(1)}, u32[]{:S(2)}, u32[]{:S(2)}) %collective-permute-start.1) | collective-permute-done | bytes 589856 | tf_op jit(solution)/shard_map/ppermute | solution.py:19
  (68 shorter events, 23.8 us)
Async XLA Ops:
  7.2 5.0 %copy-start = (s32[384]{0:T(512)S(1)}, s32[384]{0:T(512)}, u32[]{:S(2)}) copy-start(s32[384]{0:T(512)} %param.7) | copy-start | bytes 4612
  7.2 130.0 %all-gather.2.cloned.1.call-start = ((), (), s32[]{:S(2)}) async-start(), calls=%async_computation.3 | async-start | bytes 19464192 | tf_op jit(solution)/shard_map/all_gather | solution.py:122
  19.3 20.6 %all-to-all-start.1 = ((f32[128,1,1]{2,1,0:T(1,128)}), f32[128,1,1]{2,1,0:T(1,128)S(1)}, u32[]{:S(2)}, u32[]{:S(2)}) async-start(f32[128,1,1]{2,1,0:T(1,128)} %copy.9), calls=%async_computation.1 | async-start | bytes 131072 | tf_op jit(solution)/shard_map/all_to_all | solution.py:93
  39.9 68.2 %all-to-all-start = ((f32[128,1,4608]{2,1,0:T(1,128)}), f32[128,1,4608]{2,1,0:T(1,128)S(1)}, u32[]{:S(2)}, u32[]{:S(2)}) async-start(f32[128,1,4608]{2,1,0:T(1,128)} %copy.8), calls=%async_computation | async-start | bytes 4718592 | tf_op jit(solution)/shard_map/all_to_all | solution.py:86
  49.7 263.5 %reduce-scatter.2.cloned.1.call-start = ((), (), s32[]{:S(2)}) async-start(), calls=%async_computation.4 | async-start | bytes 19464192 | tf_op jit(solution)/shard_map/reduce_scatter | solution.py:131
  108.1 2.3 copy-start.1
  130.9 3.2 collective-permute-start
  158.9 1.0 copy-start.3
  167.0 1.0 copy-start.3
  175.1 1.0 copy-start.3
  183.2 1.0 copy-start.3
  195.8 118.6 %copy-start.2 = (bf16[1,64,4608]{2,1,0:T(8,128)(2,1)S(1)}, bf16[1,64,4608]{2,1,0:T(8,128)(2,1)}, u32[]{:S(2)}) copy-start(bf16[1,64,4608]{2,1,0:T(8,128)(2,1)} %param.9) | copy-start | bytes 1769476
  195.8 118.6 %copy-start.4 = (f32[4608]{0:T(1024)S(1)}, f32[4608]{0:T(1024)}, u32[]{:S(2)}) copy-start(f32[4608]{0:T(1024)} %get-tuple-element.39) | copy-start | bytes 55300
  315.8 15.3 %collective-permute-start.1 = (bf16[64,4608]{1,0:T(8,128)(2,1)S(1)}, bf16[64,4608]{1,0:T(8,128)(2,1)S(1)}, u32[]{:S(2)}, u32[]{:S(2)}) collective-permute-start(bf16[64,4608]{1,0:T(8,128)(2,1)S(1)} %fusion.21), channel_id=1, source_target_pairs={{0,32},{32,64},{64,96},{96,0},{1,33},{33,65},{65,97},{97,1},{2,34}... | collective-permute-start | bytes 1769480 | tf_op jit(solution)/shard_map/ppermute | solution.py:19
Sparse Core Ops, SparseCore 0:
  12.3 105.5 all-gather.1
  196.0 117.1 reduce-scatter.1
where the time goes:
time: 340 us; the launch traced here: 339 us
  waiting for transfers between devices  173 us (51%)
  local copies, waits for them, and re-layouts  50.9 us (15%)
  matrix products  39.4 us (12%)
  other arithmetic  30.2 us (9%)
  starting transfers between devices  22.7 us (7%)
  between operations  14.3 us (4%)
  loops' own time  8.37 us (2%)
    reduce_scatter x1, waiting for transfers between devices, body(): lax.psum_scatter(jnp.dot(attended, output_rows, preferred_element_type=jn...  117 us
    all_to_all x1, waiting for transfers between devices, body(): lax.all_to_all(moving.reshape(devices, peer_rows, model_width), ('section...  38.7 us
    dot_general x1, matrix products, body(): lax.dot_general(lax.all_gather(scaled, 'dp', axis=0, tiled=True), project...  14.9 us
    ppermute x1, waiting for transfers between devices, passed_along(): lax.ppermute(shard, axis, [(i, (i + by) % size) for i in range(size)])  13.7 us
    gather x1, local copies, waits for them, and re-layouts, body(): master = gathered_rows[jnp.argsort(places)]  12.2 us
    all_to_all x1, starting transfers between devices, body(): lax.all_to_all(labels.reshape(devices, peer_rows), ('section', 'dp'), spl...  11.1 us
    dot_general x1, matrix products, body(): jnp.dot(attended, output_rows, preferred_element_type=jnp.float32)  10.1 us
    all_to_all x1, starting transfers between devices, body(): lax.all_to_all(moving.reshape(devices, peer_rows, model_width), ('section...  9.74 us
  transfers between devices with their start and end apart: 6, of which 4 were waited for; matrix products, arithmetic and copies ran while one was open for 18% of the time, Pallas kernels for 0%

commit v1 on v0

v1 whole, which is shorter than its diff:
```python
import jax
import jax.numpy as jnp
from jax import lax
from jax.experimental import pallas as pl
from jax.experimental.pallas import tpu as pltpu
from jax.sharding import PartitionSpec as P

MESH = pl.DeviceIdType.MESH
F32 = jnp.float32
BF16 = jnp.bfloat16

D = 4608
HD = 128
SLAB = 384
TOK = 2048
OWN_TOK = 64
HALF = D // 2
COLOR = HALF // 2
QUARTER = D // 4
DEVICES = 128
LABEL = SLAB
WIDE = D + LABEL
TILE = 384
QB = 256

epsilon = 1e-06
LOG2E = 1.4426950408889634
score_scale = LOG2E / 12.0

NT_DIMS = (((1,), (1,)), ((), ()))
TN_DIMS = (((0,), (0,)), ((), ()))


def iota(shape, dim):
    return lax.broadcasted_iota(jnp.int32, shape, dim)


def one_hot(mask):
    return jnp.where(mask, 1.0, 0.0).astype(BF16)


def mm(a, b, dims=None):
    if dims is None:
        return jnp.dot(a, b, preferred_element_type=F32)
    return lax.dot_general(a, b, dims, preferred_element_type=F32)


def span(index, size):
    return pl.ds(pl.multiple_of(index * size, size), size)


def layer_kernel(
    old_hbm, rows_ref, gains_ref, hid_ref, upd_ref, arr_hbm,
    stage, old_b, s0, b1, s1, b2, s2, b3, s3, b4, w, wp, nrm, xg, pown, psend, precv, z_qkv,
    att, hg, of, ow, sc, ps, rh, rf, mx, mixed, load_sem, loc_sem, send_sem, recv_sem,
):
    y = lax.axis_index("section")
    d = lax.axis_index("dp")
    c = lax.rem(d, 2)
    chip = lax.div(d, 2)
    x = lax.rem(chip, 4)
    z = lax.div(chip, 4)
    me = y * 32 + d

    def at(zz, xx, cc, yy=y):
        return (yy, (lax.rem(zz + 4, 4) * 4 + lax.rem(xx + 4, 4)) * 2 + cc)

    partner = at(z, x, 1 - c)
    ids = {}
    sent = []

    def slot(key):
        return ids.setdefault(key, len(ids))

    def send(key, src, dst, dev):
        n = slot(key)
        copy = pltpu.make_async_remote_copy(
            src_ref=src, dst_ref=dst, send_sem=send_sem.at[n], recv_sem=recv_sem.at[n],
            device_id=dev, device_id_type=MESH,
        )
        copy.start()
        sent.append(copy)

    def receive(key, dst):
        n = slot(key)
        pltpu.make_async_remote_copy(
            src_ref=dst, dst_ref=dst, send_sem=send_sem.at[n], recv_sem=recv_sem.at[n],
            device_id=partner, device_id_type=MESH,
        ).wait_recv()

    local_count = [0]

    def local(src, dst):
        copy = pltpu.make_async_copy(src, dst, loc_sem.at[local_count[0]])
        local_count[0] += 1
        copy.start()
        return copy

    def load(i):
        return pltpu.make_async_copy(
            old_hbm.at[pl.ds(i * 128, 128)], stage.at[i % 2], load_sem.at[i % 2]
        )

    load(0).start()
    load(1).start()

    barrier = pltpu.get_barrier_semaphore()
    greeted = [partner]
    for k in (1, 2, 3):
        greeted += [at(z, x, c, lax.rem(y + k, 4)), at(z + k, x, c), at(z, x + k, c)]
    for dev in greeted:
        pl.semaphore_signal(barrier, inc=1, device_id=dev, device_id_type=MESH)

    h = hid_ref[...].astype(F32)
    scale = lax.rsqrt(jnp.mean(h * h, axis=-1, keepdims=True) + epsilon)
    nrm[...] = (h * scale * gains_ref[0:1, :]).astype(BF16)
    pl.semaphore_wait(barrier, len(greeted))

    own_rows = pl.ds(pl.multiple_of(chip * 128 + c * 64, 64), 64)
    other_rows = pl.ds(pl.multiple_of(chip * 128 + (1 - c) * 64, 64), 64)
    send("norm", nrm.at[:, span(1 - c, HALF)], xg.at[own_rows], partner)
    own_copy = local(nrm.at[:, span(c, HALF)], xg.at[own_rows])

    def ag_place(colour, fk, sk, half):
        if colour == 0:
            cc = lax.rem(z + sk + 4, 4) * 4 + lax.rem(x + fk + 4, 4)
        else:
            cc = lax.rem(z + fk + 4, 4) * 4 + lax.rem(x + sk + 4, 4)
        if half is None:
            rows = pl.ds(pl.multiple_of(cc * 128, 128), 128)
        else:
            rows = pl.ds(pl.multiple_of(cc * 128 + half * 64, 64), 64)
        return xg.at[rows, pl.ds(colour * COLOR, COLOR)]

    def ag_send(colour, axis, step, fk, sk, half=None):
        along_x = (axis == "f") == (colour == 0)
        dev = at(z, x + step, c) if along_x else at(z + step, x, c)
        ref = ag_place(colour, fk, sk, half)
        send(("ag", colour, axis, step, fk % 4, sk % 4, half), ref, ref, dev)

    def ag_recv(colour, axis, step, fk, sk, half=None):
        key = ("ag", colour, axis, step, fk % 4, sk % 4, half)
        if axis == "f":
            fk = (fk - step) % 4
        else:
            sk = (sk - step) % 4
        receive(key, ag_place(colour, fk, sk, half))

    def part(step):
        return 0 if step == 1 else 1

    both = [(colour, step) for colour in (0, 1) for step in (1, -1)]

    own_copy.wait()
    receive("norm", xg.at[other_rows])
    for colour, step in both:
        ag_send(colour, "f", step, 0, 0)
    for colour, step in both:
        ag_send(colour, "s", step, 0, 0)

    rows = rows_ref[...]
    owner = jnp.floor((rows.astype(F32) + 0.5) * (1.0 / SLAB)).astype(jnp.int32)
    place = rows - owner * SLAB
    dest = iota((DEVICES, SLAB), 0)
    choose = one_hot((owner == dest) & (dest != me))
    place_t = one_hot(place == iota((SLAB, SLAB), 0))
    keep_t = one_hot((rows - me * SLAB) == iota((SLAB, SLAB), 0))
    for i in range(3):
        load(i).wait()

        def cast(j, carry):
            at_rows = pl.ds(pl.multiple_of(j * 16, 16), 16)
            old_b[pl.ds(pl.multiple_of(i * 128 + j * 16, 16), 16), :] = stage[i % 2, at_rows, :].astype(BF16)
            return carry

        lax.fori_loop(0, 8, cast, 0)
        if i == 0:
            load(2).start()

    def tiles(count, body):
        def one(j, carry):
            body(span(j, TILE))
            return carry

        lax.fori_loop(0, count, one, 0)

    def choose_rows(cols):
        s0[:, cols] = mm(choose, old_b[:, cols]).astype(BF16)

    tiles(D // TILE, choose_rows)
    s0[:, D:] = mm(choose, place_t, NT_DIMS).astype(BF16)

    def exchange_start(name, src, dst, index, dev):
        for k in (1, 2, 3):
            send((name, k), src.at[span(lax.rem(index + k, 4), 32)], dst.at[span(index, 32)], dev(k))
        return local(src.at[span(index, 32)], dst.at[span(index, 32)])

    def exchange_wait(name, dst, index, own):
        own.wait()
        for k in (1, 3, 2):
            receive((name, k), dst.at[span(lax.rem(index + 4 - k, 4), 32)])

    def regroup(src, dst, source_row):
        r = iota((DEVICES, DEVICES), 0)
        perm = one_hot(iota((DEVICES, DEVICES), 1) == source_row(r))

        def move(cols):
            dst[:, cols] = mm(perm, src[:, cols]).astype(BF16)

        tiles(WIDE // TILE, move)

    own_y = exchange_start("y", s0, b1, y, lambda k: at(z, x, c, lax.rem(y + k, 4)))

    for colour, step in both:
        ag_recv(colour, "f", step, 0, 0)
        ag_send(colour, "f", step, -step, 0, part(step))
        for step2 in (1, -1):
            ag_send(colour, "s", step2, -step, 0)
    for colour, step in both:
        ag_recv(colour, "s", step, 0, 0)
        ag_send(colour, "s", step, 0, -step, part(step))

    exchange_wait("y", b1, y, own_y)
    regroup(b1, s1, lambda r: ((r >> 3) & 3) * 32 + (r >> 5) * 8 + (r & 7))
    own_z = exchange_start("z", s1, b2, z, lambda k: at(z + k, x, c))

    for colour in (0, 1):
        for step in (1, -1):
            ag_recv(colour, "f", step, -step, 0, part(step))
        for step in (1, -1):
            ag_send(colour, "s", step, 2, 0)

    exchange_wait("z", b2, z, own_z)
    regroup(b2, s2, lambda r: ((r >> 3) & 3) * 32 + ((r >> 1) & 3) * 8 + (r >> 5) * 2 + (r & 1))
    own_x = exchange_start("x", s2, b3, x, lambda k: at(z, x + k, c))

    for fk in (-1, 1):
        for colour, step in both:
            ag_recv(colour, "s", step, fk, 0)
            ag_send(colour, "s", step, fk, -step, part(step))

    exchange_wait("x", b3, x, own_x)
    regroup(b3, s3, lambda r: (r & 63) * 2 + (r >> 6))
    send("core", s3.at[span(1 - c, 64)], b4.at[span(c, 64)], partner)
    own_c = local(s3.at[span(c, 64)], b4.at[span(c, 64)])

    for colour, step in both:
        ag_recv(colour, "s", step, 2, 0)
        ag_send(colour, "s", step, 2, -step, part(step))

    own_c.wait()
    receive("core", b4.at[span(1 - c, 64)])
    arr_copy = local(b4, arr_hbm)

    arrived = b4[:, D:]

    def place_rows(cols):
        w[:, cols] = (
            mm(keep_t, old_b[:, cols]) + mm(arrived, b4[:, cols], TN_DIMS)
        ).astype(BF16)

    tiles(D // TILE, place_rows)

    theirs = span(1 - c, HALF)
    ours = span(c, HALF)
    k_rows = pl.ds(pl.multiple_of(256 + 64 * c, 64), 64)
    v_rows = pl.ds(pl.multiple_of(384 + 64 * c, 64), 64)
    k_rows_p = pl.ds(pl.multiple_of(256 + 64 * (1 - c), 64), 64)
    v_rows_p = pl.ds(pl.multiple_of(384 + 64 * (1 - c), 64), 64)
    o_rows = span(c, 128)
    o_rows_p = span(1 - c, 128)
    send("wq", w.at[0:128, theirs], wp.at[128:256], partner)
    send("wk", w.at[128:192, theirs], wp.at[k_rows], partner)
    send("wv", w.at[192:256, theirs], wp.at[v_rows], partner)
    send("wo", w.at[256:384], of.at[o_rows], partner)
    own_w = [
        local(w.at[0:128, ours], wp.at[0:128]),
        local(w.at[128:192, ours], wp.at[k_rows]),
        local(w.at[192:256, ours], wp.at[v_rows]),
        local(w.at[256:384], of.at[o_rows]),
    ]

    for fk in (0, -1, 1, 2):
        for colour, step in both:
            ag_recv(colour, "s", step, fk, -step, part(step))

    for copy in own_w:
        copy.wait()
    receive("wq", wp.at[128:256])
    receive("wk", wp.at[k_rows_p])
    receive("wv", wp.at[v_rows_p])
    receive("wo", of.at[o_rows_p])

    fi = x + c * (z - x)
    si = z + c * (x - z)

    def along_f(k):
        return at(z + c * k, x + (1 - c) * k, c)

    def along_s(k):
        return at(z + (1 - c) * k, x + c * k, c)

    for k in (1, 3, 2):
        send(("ow", k), of.at[:, span(lax.rem(fi + k, 4), QUARTER)], ow.at[fi], along_f(k))
    own_o = local(of.at[:, span(fi, QUARTER)], ow.at[fi])

    group = 512

    def project(g):
        at_rows = pl.ds(g * group, group)
        acc = mm(xg[at_rows, :], wp[...], NT_DIMS)
        pown[at_rows, 0:128] = acc[:, 0:128]
        pown[at_rows, 128:384] = acc[:, 256:512]
        psend[at_rows, :] = acc[:, 128:512].astype(BF16)

    for g in range(TOK // group):
        project(g)
        at_rows = pl.ds(g * group, group)
        send(("proj", g), psend.at[at_rows], precv.at[at_rows], partner)

    def combine(g):
        at_rows = pl.ds(g * group, group)
        receive(("proj", g), precv.at[at_rows])
        z_qkv[at_rows, :] = (pown[at_rows, :] + precv[at_rows, :].astype(F32)).astype(BF16)

    def attend(qb):
        q = z_qkv[qb * QB : (qb + 1) * QB, 0:128]
        peak = None
        for kb in range(qb + 1):
            cols = slice(kb * QB, (kb + 1) * QB)
            s = mm(q, z_qkv[cols, 128:256], NT_DIMS) * score_scale
            if kb == qb:
                s = jnp.where(iota((QB, QB), 0) >= iota((QB, QB), 1), s, -1e30)
            sc[qb % 2, :, cols] = s
            top = jnp.maximum(s[:, 0:128], s[:, 128:256])
            peak = top if peak is None else jnp.maximum(peak, top)
        peak = jnp.max(peak, axis=-1, keepdims=True)
        total = None
        out = None
        for kb in range(qb + 1):
            cols = slice(kb * QB, (kb + 1) * QB)
            e = jnp.exp2(sc[qb % 2, :, cols] - peak)
            add = e[:, 0:128] + e[:, 128:256]
            total = add if total is None else total + add
            o = mm(e.astype(BF16), z_qkv[cols, 256:384])
            out = o if out is None else out + o
        total = jnp.sum(total, axis=-1, keepdims=True)
        out = (out / total).astype(BF16)
        for i in range(QB // 128):
            ci = qb * (QB // 128) + i
            turned = (ci % 4) * 4 + ci // 4
            att[0, ci * 64 : ci * 64 + 64, :] = out[i * 128 : i * 128 + 64]
            att[1, turned * 64 : turned * 64 + 64, :] = out[i * 128 + 64 : i * 128 + 128]

    for g in range(TOK // group):
        combine(g)
    for qb in range(TOK // QB):
        attend(qb)

    head_cols = span(c, 128)
    head_cols_p = span(1 - c, 128)
    send("att", att.at[1 - c], hg.at[si, :, head_cols], partner)
    own_a = local(att.at[c], hg.at[fi, :, head_cols])
    own_a.wait()
    receive("att", hg.at[fi, :, head_cols_p])

    def f_at(k):
        return lax.rem(fi + k + 4, 4)

    for step in (1, -1):
        send(("hg", step), hg.at[fi], hg.at[fi], along_f(step))
    for step in (1, -1):
        receive(("hg", step), hg.at[f_at(-step)])
        rows_f = pl.ds(part(step) * 512, 512)
        ref = hg.at[f_at(-step), rows_f]
        send(("hg2", step), ref, ref, along_f(step))
    for step in (1, -1):
        receive(("hg2", step), hg.at[f_at(2), pl.ds(part(step) * 512, 512)])

    own_o.wait()
    for k in (1, 3, 2):
        receive(("ow", k), ow.at[lax.rem(fi + 4 - k, 4)])

    def partial(j, cols):
        sg = lax.rem(si + j + 4, 4)
        at_rows = span(sg, 256)
        acc = None
        for f in range(4):
            o = mm(hg[f, at_rows, :], ow[f, :, cols])
            acc = o if acc is None else acc + o
        return acc

    def far(cols):
        ps[0, :, cols] = partial(2, cols).astype(BF16)

    tiles(QUARTER // TILE, far)
    send(("rh", 1), ps.at[0, 0:128], rh.at[0], along_s(1))
    send(("rh", -1), ps.at[0, 128:256], rh.at[1], along_s(-1))

    receive(("rh", 1), rh.at[0])

    def plus(cols):
        acc = partial(1, cols)
        ps[1, 0:128, cols] = (acc[0:128] + rh[0, :, cols].astype(F32)).astype(BF16)
        ps[1, 128:256, cols] = acc[128:256].astype(BF16)

    tiles(QUARTER // TILE, plus)
    send(("rf", 1), ps.at[1], rf.at[0], along_s(1))

    receive(("rh", -1), rh.at[1])

    def minus(cols):
        acc = partial(-1, cols)
        ps[2, 0:128, cols] = acc[0:128].astype(BF16)
        ps[2, 128:256, cols] = (acc[128:256] + rh[1, :, cols].astype(F32)).astype(BF16)

    tiles(QUARTER // TILE, minus)
    send(("rf", -1), ps.at[2], rf.at[1], along_s(-1))

    receive(("rf", 1), rf.at[0])
    receive(("rf", -1), rf.at[1])

    def near(cols):
        acc = partial(0, cols)
        mx[:, cols] = (acc + rf[0, :, cols].astype(F32) + rf[1, :, cols].astype(F32)).astype(BF16)

    tiles(QUARTER // TILE, near)

    for k in (1, 3, 2):
        send(("mx", k), mx.at[span(lax.rem(fi + k, 4), 64)], mixed.at[:, span(fi, QUARTER)], along_f(k))
    own_m = local(mx.at[span(fi, 64)], mixed.at[:, span(fi, QUARTER)])
    own_m.wait()
    for k in (1, 3, 2):
        receive(("mx", k), mixed.at[:, span(lax.rem(fi + 4 - k, 4), QUARTER)])

    m = mixed[...].astype(F32)
    scale2 = lax.rsqrt(jnp.mean(m * m, axis=-1, keepdims=True) + epsilon)
    upd_ref[...] = (hid_ref[...].astype(F32) + m * scale2 * gains_ref[1:2, :]).astype(BF16)

    arr_copy.wait()
    for copy in sent:
        copy.wait_send()


def layer(old_master, rows, gains, hidden):
    vmem = pl.BlockSpec(memory_space=pltpu.VMEM)
    anywhere = pl.BlockSpec(memory_space=pl.ANY)
    exch = pltpu.VMEM((DEVICES, WIDE), BF16)
    return pl.pallas_call(
        layer_kernel,
        out_shape=(
            jax.ShapeDtypeStruct((OWN_TOK, D), BF16),
            jax.ShapeDtypeStruct((DEVICES, WIDE), BF16),
        ),
        in_specs=[anywhere, vmem, vmem, vmem],
        out_specs=(vmem, anywhere),
        scratch_shapes=[
            pltpu.VMEM((2, 128, D), F32),
            pltpu.VMEM((SLAB, D), BF16),
            exch, exch, exch, exch, exch, exch, exch, exch,
            pltpu.VMEM((SLAB, D), BF16),
            pltpu.VMEM((512, HALF), BF16),
            pltpu.VMEM((OWN_TOK, D), BF16),
            pltpu.VMEM((TOK, HALF), BF16),
            pltpu.VMEM((TOK, 384), F32),
            pltpu.VMEM((TOK, 384), BF16),
            pltpu.VMEM((TOK, 384), BF16),
            pltpu.VMEM((TOK, 384), BF16),
            pltpu.VMEM((2, TOK // 2, 128), BF16),
            pltpu.VMEM((4, TOK // 2, 256), BF16),
            pltpu.VMEM((256, D), BF16),
            pltpu.VMEM((4, 256, QUARTER), BF16),
            pltpu.VMEM((2, QB, TOK), F32),
            pltpu.VMEM((3, 256, QUARTER), BF16),
            pltpu.VMEM((2, 128, QUARTER), BF16),
            pltpu.VMEM((2, 256, QUARTER), BF16),
            pltpu.VMEM((256, QUARTER), BF16),
            pltpu.VMEM((OWN_TOK, D), BF16),
            pltpu.SemaphoreType.DMA((2,)),
            pltpu.SemaphoreType.DMA((16,)),
            pltpu.SemaphoreType.DMA((96,)),
            pltpu.SemaphoreType.DMA((96,)),
        ],
        compiler_params=pltpu.CompilerParams(
            collective_id=0, has_side_effects=True, vmem_limit_bytes=62 * 1024 * 1024
        ),
    )(old_master, rows, gains, hidden)


def place_kernel(old_ref, rows_ref, arr_ref, lab_ref, out_ref):
    me = lax.axis_index("section") * 32 + lax.axis_index("dp")
    keep_t = one_hot((rows_ref[...] - me * SLAB) == iota((SLAB, SLAB), 0))
    v = old_ref[...]
    hi = v.astype(BF16)
    rest = v - hi.astype(F32)
    mid = rest.astype(BF16)
    low = (rest - mid.astype(F32)).astype(BF16)
    kept = (mm(keep_t, hi) + mm(keep_t, mid)) + mm(keep_t, low)
    out_ref[...] = kept + mm(lab_ref[...], arr_ref[...], TN_DIMS)


def place_master(old_master, rows, arrived):
    width = 512
    return pl.pallas_call(
        place_kernel,
        grid=(D // width,),
        out_shape=jax.ShapeDtypeStruct((SLAB, D), F32),
        in_specs=[
            pl.BlockSpec((SLAB, width), lambda j: (0, j)),
            pl.BlockSpec((1, SLAB), lambda j: (0, 0)),
            pl.BlockSpec((DEVICES, width), lambda j: (0, j)),
            pl.BlockSpec((DEVICES, LABEL), lambda j: (0, D // LABEL)),
        ],
        out_specs=pl.BlockSpec((SLAB, width), lambda j: (0, j)),
        compiler_params=pltpu.CompilerParams(vmem_limit_bytes=32 * 1024 * 1024),
        cost_estimate=pl.CostEstimate(flops=5_000_000_000, bytes_accessed=15_000_000, transcendentals=0),
    )(old_master, rows, arrived, arrived)


def body(old_master, old_rows, gains, hidden_in):
    rows = old_rows.reshape(1, SLAB)
    updated, arrived = layer(old_master, rows, gains[0], hidden_in[0])
    size = lax.axis_size("section")
    passed = lax.ppermute(updated, "section", [(i, (i + 1) % size) for i in range(size)])
    master = place_master(old_master, rows, arrived)
    return (master, passed[None])


def solution(mesh):
    in_specs = (
        P(("section", "dp"), None),
        P(("section", "dp")),
        P("section", None, None),
        P("section", "dp", None),
    )
    out_specs = (P(("section", "dp"), None), P("section", "dp", None))
    return jax.shard_map(body, mesh=mesh, in_specs=in_specs, out_specs=out_specs, check_vma=False)
```

time: 340 us -> 166 us (0.49)
  waiting for transfers between devices: 173 us -> 0.01 us
  Pallas kernels: 0 us -> 158 us
  local copies, waits for them, and re-layouts: 50.9 us -> 6.38 us
  matrix products: 39.4 us -> 0 us
  other arithmetic: 30.2 us -> 0 us
  starting transfers between devices: 22.7 us -> 0.59 us
  between operations: 14.3 us -> 0.64 us
  loops' own time: 8.37 us -> 0 us
    pallas_call x0 -> x2, Pallas kernels: none -> 158 us  [the longest x1 148 us: layer(): pl.pallas_call(layer_kernel, out_shape=(jax.ShapeDtypeStruct((OWN_TOK, D)...]
    reduce_scatter x1 -> x0, waiting for transfers between devices: 117 us -> none  [body(): lax.psum_scatter(jnp.dot(attended, output_rows, preferred_element_type=jn...]
    dot_general x10 -> x0, matrix products: 39.4 us -> none  [the longest x1 14.9 us: body(): lax.dot_general(lax.all_gather(scaled, 'dp', axis=0, tiled=True), project...]
    all_to_all x2 -> x0, waiting for transfers between devices: 38.7 us -> none  [the longest x1 38.7 us: body(): lax.all_to_all(moving.reshape(devices, peer_rows, model_width), ('section...]
    gather x7 -> x0, local copies, waits for them, and re-layouts: 33.5 us -> none  [the longest x1 12.2 us: body(): master = gathered_rows[jnp.argsort(places)]]
    all_to_all x2 -> x0, starting transfers between devices: 20.9 us -> none  [the longest x1 11.1 us: body(): lax.all_to_all(labels.reshape(devices, peer_rows), ('section', 'dp'), spl...]
    ppermute x2 -> x1, waiting for transfers between devices: 16.8 us -> 0.01 us  [body(): lax.ppermute(updated, 'section', [(i, (i + 1) % size) for i in range(size)])]
    another operation x1 -> x0, loops' own time: 8.37 us -> none  [attend(): return lax.map(one_block, starts).reshape(length, value_cols.shape[1])]
  transfers between devices with their start and end apart: 6 -> 1, of which waited for: 4 -> 0; matrix products, arithmetic and copies ran while one was open for 18% -> 0% of each run, Pallas kernels for 0% -> 6%
where the time goes in v1:
time: 166 us
  Pallas kernels  158 us (95%)
  local copies, waits for them, and re-layouts  6.38 us (4%)
    pallas_call x1, Pallas kernels, layer(): pl.pallas_call(layer_kernel, out_shape=(jax.ShapeDtypeStruct((OWN_TOK, D)...  148 us
    pallas_call x1, Pallas kernels, place_master(): pl.pallas_call(place_kernel, grid=(D // width,), out_shape=jax.ShapeDtype...  10.2 us
    unnamed x7, local copies, waits for them, and re-layouts  5.13 us
  transfers between devices with their start and end apart: 1, of which 0 were waited for; matrix products, arithmetic and copies ran while one was open for 0% of the time, Pallas kernels for 6%

profile of v1, /device:TPU:0, one launch (start us, length us, event | category | flops | bytes accessed | tf_op | source)
XLA Modules:
  0.0 165.8 jit_solution(9518154848926918998)
XLA Ops:
  0.6 1.2 reshape.7.rows_ref
  1.9 0.0 copy-start.1
  1.9 148.0 %shard_map.59 = (bf16[64,4608]{1,0:T(8,128)(2,1)}, bf16[128,4992]{1,0:T(8,128)(2,1)}) custom-call(f32[384,4608]{1,0:T(8,128)} %old_ref.1, s32[1,384]{1,0:T(1,128)} %reshape.7.rows_ref, f32[2,4608]{1,0:T(2,128)} %bitcast.5, bf16[64,4608]{1,0:T(8,128)(2,1)} %bitcast.4), custom_call_target="tpu_custom_call" | custom-call | tf_op jit(solution)/shard_map/pallas_call | solution.py:449
  149.9 0.6 collective-permute-start
  150.5 0.0 copy-done.1
  150.5 0.0 copy-start
  150.5 3.0 %copy-done = f32[384,4608]{1,0:T(8,128)S(1)} copy-done((f32[384,4608]{1,0:T(8,128)S(1)}, f32[384,4608]{1,0:T(8,128)}, u32[]{:S(2)}) %copy-start) | copy-done | bytes 7077912
  153.5 0.0 copy-start.2
  153.5 1.3 copy-done.2
  154.8 10.2 %shard_map.60 = f32[384,4608]{1,0:T(8,128)} custom-call(f32[384,4608]{1,0:T(8,128)S(1)} %copy-done, s32[1,384]{1,0:T(1,128)S(1)} %copy-done.1, bf16[128,4992]{1,0:T(8,128)(2,1)S(1)} %copy-done.2, bf16[128,4992]{1,0:T(8,128)(2,1)S(1)} %copy-done.2), custom_call_target="tpu_custom_call" | custom-call | flops 5000000000 | bytes 15000000 | tf_op jit(solution)/shard_map/pallas_call | solution.py:504
  165.0 0.0 collective-permute-done
  165.0 0.8 copy.7
Async XLA Ops:
  1.9 148.6 %copy-start.1 = (s32[1,384]{1,0:T(1,128)S(1)}, s32[1,384]{1,0:T(1,128)}, u32[]{:S(2)}) copy-start(s32[1,384]{1,0:T(1,128)} %reshape.7.rows_ref) | copy-start | bytes 4612
  149.9 15.1 %collective-permute-start = (bf16[64,4608]{1,0:T(8,128)(2,1)}, bf16[64,4608]{1,0:T(8,128)(2,1)S(1)}, u32[]{:S(2)}, u32[]{:S(2)}) collective-permute-start(bf16[64,4608]{1,0:T(8,128)(2,1)} %get-tuple-element.5), channel_id=1, source_target_pairs={{0,32},{32,64},{64,96},{96,0},{1,33},{33,65},{65,97},{97,1},{2,34}... | collective-permute-start | bytes 1769480 | tf_op jit(solution)/shard_map/ppermute | solution.py:524
  150.5 3.0 %copy-start = (f32[384,4608]{1,0:T(8,128)S(1)}, f32[384,4608]{1,0:T(8,128)}, u32[]{:S(2)}) copy-start(f32[384,4608]{1,0:T(8,128)} %old_ref.1) | copy-start | bytes 21233668
  153.5 1.3 copy-start.2

commit v2 on v1

v2 whole, which is shorter than its diff:
```python
import jax
import jax.numpy as jnp
from jax import lax
from jax.experimental import pallas as pl
from jax.experimental.pallas import tpu as pltpu
from jax.sharding import PartitionSpec as P

MESH = pl.DeviceIdType.MESH
F32 = jnp.float32
BF16 = jnp.bfloat16

D = 4608
HD = 128
SLAB = 384
TOK = 2048
OWN_TOK = 64
HALF = D // 2
COLOR = HALF // 2
QUARTER = D // 4
DEVICES = 128
PIECE = HALF + 128
TILE = 384
GROUP = 512
QB = 256

epsilon = 1e-06
LOG2E = 1.4426950408889634
score_scale = LOG2E / 12.0

NT_DIMS = (((1,), (1,)), ((), ()))
TN_DIMS = (((0,), (0,)), ((), ()))


def iota(shape, dim):
    return lax.broadcasted_iota(jnp.int32, shape, dim)


def one_hot(mask):
    return jnp.where(mask, 1.0, 0.0).astype(BF16)


def mm(a, b, dims=None):
    if dims is None:
        return jnp.dot(a, b, preferred_element_type=F32)
    return lax.dot_general(a, b, dims, preferred_element_type=F32)


def span(index, size):
    return pl.ds(pl.multiple_of(index * size, size), size)


def merge(left, right):
    n = left.shape[1]
    pair = jnp.concatenate([left.reshape(16, 8, n), right.reshape(16, 8, n)], axis=1)
    return pair.reshape(256, n).astype(BF16)


def layer_kernel(
    old_hbm, rows_ref, gains_ref, hid_ref, master_hbm, out_ref,
    old_f, old_b, s1, b1, s2, b3, w, wp, nrm, xg, acc, psend, precv, z_qkv,
    att, hg, of, ow, sc, part_f, ps, rh, rf, mx, mixed, hid_y, gains_y,
    load_sem, loc_sem, send_sem, recv_sem,
):
    y = lax.axis_index("section")
    d = lax.axis_index("dp")
    c = lax.rem(d, 2)
    chip = lax.div(d, 2)
    x = lax.rem(chip, 4)
    z = lax.div(chip, 4)
    me = y * 32 + d

    def at(zz, xx, cc, yy=y):
        return (lax.rem(yy + 4, 4), (lax.rem(zz + 4, 4) * 4 + lax.rem(xx + 4, 4)) * 2 + cc)

    partner = at(z, x, 1 - c)
    ids = {}
    sent = []

    def slot(key):
        return ids.setdefault(key, len(ids))

    def send(key, src, dst, dev):
        n = slot(key)
        copy = pltpu.make_async_remote_copy(
            src_ref=src, dst_ref=dst, send_sem=send_sem.at[n], recv_sem=recv_sem.at[n],
            device_id=dev, device_id_type=MESH,
        )
        copy.start()
        sent.append(copy)

    def receive(key, dst):
        n = slot(key)
        pltpu.make_async_remote_copy(
            src_ref=dst, dst_ref=dst, send_sem=send_sem.at[n], recv_sem=recv_sem.at[n],
            device_id=partner, device_id_type=MESH,
        ).wait_recv()

    local_count = [0]

    def local(src, dst):
        copy = pltpu.make_async_copy(src, dst, loc_sem.at[local_count[0]])
        local_count[0] += 1
        copy.start()
        return copy

    def load(i):
        at_rows = pl.ds(i * 128, 128)
        return pltpu.make_async_copy(old_hbm.at[at_rows], old_f.at[at_rows], load_sem.at[i])

    for i in range(3):
        load(i).start()

    barrier = pltpu.get_barrier_semaphore()
    greeted = [at(z + j, x, c, y + i) for i in range(4) for j in range(4) if i or j]
    greeted += [at(z, x, 1 - c)]
    for k in (1, 2, 3):
        greeted += [at(z, x + k, c), at(z, x + k, 1 - c), at(z, x + k, c, y + 1), at(z, x + k, c, y + 3)]
    for dev in greeted:
        pl.semaphore_signal(barrier, inc=1, device_id=dev, device_id_type=MESH)

    h = hid_ref[...].astype(F32)
    scale = lax.rsqrt(jnp.mean(h * h, axis=-1, keepdims=True) + epsilon)
    nrm[...] = (h * scale * gains_ref[0:1, :]).astype(BF16)
    pl.semaphore_wait(barrier, len(greeted))

    own_rows = pl.ds(pl.multiple_of(chip * 128 + c * 64, 64), 64)
    other_rows = pl.ds(pl.multiple_of(chip * 128 + (1 - c) * 64, 64), 64)
    send("norm", nrm.at[:, span(1 - c, HALF)], xg.at[own_rows], partner)
    own_copy = local(nrm.at[:, span(c, HALF)], xg.at[own_rows])

    def ag_place(colour, fk, sk, half):
        if colour == 0:
            cc = lax.rem(z + sk + 4, 4) * 4 + lax.rem(x + fk + 4, 4)
        else:
            cc = lax.rem(z + fk + 4, 4) * 4 + lax.rem(x + sk + 4, 4)
        if half is None:
            rows = pl.ds(pl.multiple_of(cc * 128, 128), 128)
        else:
            rows = pl.ds(pl.multiple_of(cc * 128 + half * 64, 64), 64)
        return xg.at[rows, pl.ds(colour * COLOR, COLOR)]

    def ag_send(colour, axis, step, fk, sk, half=None):
        along_x = (axis == "f") == (colour == 0)
        dev = at(z, x + step, c) if along_x else at(z + step, x, c)
        ref = ag_place(colour, fk, sk, half)
        send(("ag", colour, axis, step, fk % 4, sk % 4, half), ref, ref, dev)

    def ag_recv(colour, axis, step, fk, sk, half=None):
        key = ("ag", colour, axis, step, fk % 4, sk % 4, half)
        if axis == "f":
            fk = (fk - step) % 4
        else:
            sk = (sk - step) % 4
        receive(key, ag_place(colour, fk, sk, half))

    def part(step):
        return 0 if step == 1 else 1

    both = [(colour, step) for colour in (0, 1) for step in (1, -1)]

    def tiles(count, body, size=TILE):
        def one(j, carry):
            body(span(j, size))
            return carry

        lax.fori_loop(0, count, one, 0)

    own_copy.wait()
    receive("norm", xg.at[other_rows])
    for colour, step in both:
        ag_send(colour, "f", step, 0, 0)
    for colour, step in both:
        ag_send(colour, "s", step, 0, 0)

    rows = rows_ref[...]
    owner = jnp.floor((rows.astype(F32) + 0.5) * (1.0 / SLAB)).astype(jnp.int32)
    place = rows - owner * SLAB
    dest = iota((DEVICES, SLAB), 0)
    choose = one_hot((owner == dest) & (dest != me))
    keep_t = one_hot((rows - me * SLAB) == iota((SLAB, SLAB), 0))
    low_t = one_hot((place & 127) == iota((128, SLAB), 0))
    high_t = one_hot((place >> 7) == iota((128, SLAB), 0))
    for i in range(3):
        load(i).wait()

        def cast(j, carry):
            at_rows = pl.ds(pl.multiple_of(i * 128 + j * 16, 16), 16)
            old_b[at_rows, :] = old_f[at_rows, :].astype(BF16)
            return carry

        lax.fori_loop(0, 8, cast, 0)

    def choose_rows(j, carry):
        cols = span(j, TILE)
        cols2 = pl.ds(pl.multiple_of(HALF + j * TILE, TILE), TILE)
        s1[:, cols] = merge(mm(choose, old_b[:, cols]), mm(choose, old_b[:, cols2]))
        return carry

    lax.fori_loop(0, HALF // TILE, choose_rows, 0)
    s1[:, HALF:] = merge(mm(choose, low_t, NT_DIMS), mm(choose, high_t, NT_DIMS))

    group_me = y * 4 + z
    across = [(i, j) for i in (2, 1, 3, 0) for j in (2, 1, 3, 0) if i or j]
    for i, j in across:
        g = lax.rem(y + i, 4) * 4 + lax.rem(z + j, 4)
        send(("yz", i, j), s1.at[span(g, 16)], b1.at[span(group_me, 16)], at(z + j, x, c, y + i))
    own_yz = local(s1.at[span(group_me, 16)], b1.at[span(group_me, 16)])

    send("hid", hid_ref, hid_y, at(z, x, c, y + 1))
    send("gains", gains_ref, gains_y, at(z, x, c, y + 1))

    def keep_rows(cols):
        high = old_b[:, cols]
        rest = old_f[:, cols] - high.astype(F32)
        mid = rest.astype(BF16)
        low = (rest - mid.astype(F32)).astype(BF16)
        old_f[:, cols] = (mm(keep_t, high) + mm(keep_t, mid)) + mm(keep_t, low)

    lax.fori_loop(0, 6, lambda j, t: (keep_rows(span(j, TILE)), t)[1], 0)

    for colour, step in both:
        ag_recv(colour, "f", step, 0, 0)
        ag_send(colour, "f", step, -step, 0, part(step))
        for step2 in (1, -1):
            ag_send(colour, "s", step2, -step, 0)
    for colour, step in both:
        ag_recv(colour, "s", step, 0, 0)
        ag_send(colour, "s", step, 0, -step, part(step))

    lax.fori_loop(6, D // TILE, lambda j, t: (keep_rows(span(j, TILE)), t)[1], 0)

    own_yz.wait()
    for i, j in across:
        g = lax.rem(y + 4 - i, 4) * 4 + lax.rem(z + 4 - j, 4)
        receive(("yz", i, j), b1.at[span(g, 16)])

    r2 = iota((DEVICES, 256), 0)
    from_row = (r2 & 15) * 16 + (r2 >> 4)
    perm_l = one_hot(iota((DEVICES, 256), 1) == from_row)
    perm_r = one_hot(iota((DEVICES, 256), 1) == from_row + 8)

    def regroup(j, carry):
        cols = span(j, TILE)
        cols2 = pl.ds(pl.multiple_of(HALF + j * TILE, TILE), TILE)
        piece = b1[:, cols]
        s2[:, cols] = mm(perm_l, piece).astype(BF16)
        s2[:, cols2] = mm(perm_r, piece).astype(BF16)
        return carry

    lax.fori_loop(0, HALF // TILE, regroup, 0)
    s2[:, D : D + 128] = mm(perm_l, b1[:, HALF:]).astype(BF16)
    s2[:, D + 128 :] = mm(perm_r, b1[:, HALF:]).astype(BF16)

    e_me = x * 2 + c
    for m in (4, 3, 5, 2, 6, 1, 7):
        e = lax.rem(e_me + m, 8)
        send(("xc", m), s2.at[span(e, 16)], b3.at[span(e_me, 16)], at(z, lax.div(e, 2), lax.rem(e, 2)))
    own_xc = local(s2.at[span(e_me, 16)], b3.at[span(e_me, 16)])

    for colour in (0, 1):
        for step in (1, -1):
            ag_recv(colour, "f", step, -step, 0, part(step))
        for step in (1, -1):
            ag_send(colour, "s", step, 2, 0)
    for fk in (-1, 1):
        for colour, step in both:
            ag_recv(colour, "s", step, fk, 0)
            ag_send(colour, "s", step, fk, -step, part(step))

    own_xc.wait()
    for m in (4, 3, 5, 2, 6, 1, 7):
        receive(("xc", m), b3.at[span(lax.rem(e_me + 8 - m, 8), 16)])

    low_lab = b3[:, D : D + 128]
    high_lab = b3[:, D + 128 :]
    arrived = jnp.concatenate([low_lab * high_lab[:, a : a + 1] for a in range(3)], axis=1)

    def place_rows(cols):
        m = old_f[:, cols] + mm(arrived, b3[:, cols], TN_DIMS)
        old_f[:, cols] = m
        w[:, cols] = m.astype(BF16)

    tiles(D // TILE, place_rows)
    master_copy = local(old_f, master_hbm)

    theirs = span(1 - c, HALF)
    ours = span(c, HALF)
    k_rows = pl.ds(pl.multiple_of(256 + 64 * c, 64), 64)
    v_rows = pl.ds(pl.multiple_of(384 + 64 * c, 64), 64)
    k_rows_p = pl.ds(pl.multiple_of(256 + 64 * (1 - c), 64), 64)
    v_rows_p = pl.ds(pl.multiple_of(384 + 64 * (1 - c), 64), 64)
    o_rows = span(c, 128)
    o_rows_p = span(1 - c, 128)
    send("wq", w.at[0:128, theirs], wp.at[128:256], partner)
    send("wk", w.at[128:192, theirs], wp.at[k_rows], partner)
    send("wv", w.at[192:256, theirs], wp.at[v_rows], partner)
    send("wo", w.at[256:384], of.at[o_rows], partner)
    own_w = [
        local(w.at[0:128, ours], wp.at[0:128]),
        local(w.at[128:192, ours], wp.at[k_rows]),
        local(w.at[192:256, ours], wp.at[v_rows]),
        local(w.at[256:384], of.at[o_rows]),
    ]

    for colour, step in both:
        ag_recv(colour, "s", step, 2, 0)
        ag_send(colour, "s", step, 2, -step, part(step))

    for copy in own_w:
        copy.wait()
    receive("wq", wp.at[128:256])
    receive("wk", wp.at[k_rows_p])
    receive("wv", wp.at[v_rows_p])
    receive("wo", of.at[o_rows_p])

    fi = x + c * (z - x)
    si = z + c * (x - z)

    def along_f(k, yy=y):
        return at(z + c * k, x + (1 - c) * k, c, yy)

    def along_s(k):
        return at(z + (1 - c) * k, x + c * k, c)

    for k in (2, 1, 3):
        send(("ow", k), of.at[:, span(lax.rem(fi + k, 4), QUARTER)], ow.at[fi], along_f(k))
    own_o = local(of.at[:, span(fi, QUARTER)], ow.at[fi])

    def project(colour, fk, fresh):
        if colour == 0:
            xx = lax.rem(x + fk + 4, 4)
            places = [pl.ds(pl.multiple_of((q * 4 + xx) * 128, 128), 128) for q in range(4)]
        else:
            zz = lax.rem(z + fk + 4, 4)
            places = [pl.ds(pl.multiple_of((zz * 4 + q) * 128, 128), 128) for q in range(4)]
        cols = slice(colour * COLOR, (colour + 1) * COLOR)
        block = jnp.concatenate([xg[p, cols] for p in places], axis=0)
        out = mm(block, wp[:, cols], NT_DIMS)
        for q, p in enumerate(places):
            piece = out[q * 128 : (q + 1) * 128]
            acc[p, :] = piece if fresh else acc[p, :] + piece

    for colour in (0, 1):
        for fk in (0, -1, 1, 2):
            for step in (1, -1):
                ag_recv(colour, "s", step, fk, -step, part(step))
            project(colour, fk, colour == 0)

    for g in range(4):
        at_rows = pl.ds(g * GROUP, GROUP)
        psend[at_rows, :] = acc[at_rows, 128:512].astype(BF16)
        send(("proj", g), psend.at[at_rows], precv.at[at_rows], partner)

    def combine(g):
        at_rows = pl.ds(g * GROUP, GROUP)
        receive(("proj", g), precv.at[at_rows])
        q = acc[at_rows, 0:128] + precv[at_rows, 0:128].astype(F32)
        kv = acc[at_rows, 256:512] + precv[at_rows, 128:384].astype(F32)
        z_qkv[at_rows, 0:128] = q.astype(BF16)
        z_qkv[at_rows, 128:384] = kv.astype(BF16)

    def attend(qb):
        q = z_qkv[qb * QB : (qb + 1) * QB, 0:128]
        peak = None
        for kb in range(qb + 1):
            cols = slice(kb * QB, (kb + 1) * QB)
            s = mm(q, z_qkv[cols, 128:256], NT_DIMS) * score_scale
            if kb == qb:
                s = jnp.where(iota((QB, QB), 0) >= iota((QB, QB), 1), s, -1e30)
            sc[:, cols] = s
            top = jnp.maximum(s[:, 0:128], s[:, 128:256])
            peak = top if peak is None else jnp.maximum(peak, top)
        peak = jnp.max(peak, axis=-1, keepdims=True)
        total = None
        out = None
        for kb in range(qb + 1):
            cols = slice(kb * QB, (kb + 1) * QB)
            e = jnp.exp2(sc[:, cols] - peak)
            add = e[:, 0:128] + e[:, 128:256]
            total = add if total is None else total + add
            o = mm(e.astype(BF16), z_qkv[cols, 256:384])
            out = o if out is None else out + o
        total = jnp.sum(total, axis=-1, keepdims=True)
        out = (out / total).astype(BF16)
        for i in range(QB // 128):
            ci = qb * (QB // 128) + i
            att[0, ci * 64 : ci * 64 + 64, :] = out[i * 128 : i * 128 + 64]
            att[1, ci * 64 : ci * 64 + 64, :] = out[i * 128 + 64 : i * 128 + 128]

    head_cols = span(c, 128)
    head_cols_p = span(1 - c, 128)
    own_a = {}

    def f_at(k):
        return lax.rem(fi + k + 4, 4)

    def rows_g(g, half=None):
        return pl.ds(g * 256, 256) if half is None else pl.ds(g * 256 + half * 128, 128)

    def gather_1(g):
        send(("att", g), att.at[1 - c, rows_g(g)], hg.at[si, rows_g(g), head_cols], partner)
        own_a[g] = local(att.at[c, rows_g(g)], hg.at[fi, rows_g(g), head_cols])

    def gather_2(g):
        own_a[g].wait()
        receive(("att", g), hg.at[fi, rows_g(g), head_cols_p])
        for step in (1, -1):
            ref = hg.at[fi, rows_g(g)]
            send(("hg", step, g), ref, ref, along_f(step))

    def gather_3(g):
        for step in (1, -1):
            receive(("hg", step, g), hg.at[f_at(-step), rows_g(g)])
            ref = hg.at[f_at(-step), rows_g(g, part(step))]
            send(("hg2", step, g), ref, ref, along_f(step))

    combine(0)
    attend(0)
    attend(1)
    gather_1(0)
    combine(1)
    attend(2)
    gather_2(0)
    attend(3)
    gather_1(1)
    gather_3(0)
    combine(2)
    attend(4)
    gather_2(1)
    attend(5)
    gather_1(2)
    gather_3(1)
    combine(3)
    attend(6)
    gather_2(2)
    attend(7)
    gather_1(3)
    gather_3(2)
    gather_2(3)
    gather_3(3)
    for g in range(4):
        for step in (1, -1):
            receive(("hg2", step, g), hg.at[f_at(2), rows_g(g, part(step))])

    own_o.wait()
    for k in (1, 3, 2):
        receive(("ow", k), ow.at[lax.rem(fi + 4 - k, 4)])

    def partial(j, cols):
        sg = lax.rem(si + j + 4, 4)
        out = None
        for f in range(4):
            block = jnp.concatenate(
                [
                    hg[f, pl.ds(pl.multiple_of(sg * (256 - 192 * c) + q * (64 + 192 * c), 64), 64), :]
                    for q in range(4)
                ],
                axis=0,
            )
            o = mm(block, ow[f, :, cols])
            out = o if out is None else out + o
        return out

    order = (2, 1, 3, 0)

    def piece(k, half=None):
        q = f_at(k)
        if half is None:
            return pl.ds(pl.multiple_of(q * 64, 64), 64)
        return pl.ds(pl.multiple_of(q * 64 + half * 32, 32), 32)

    def far(cols):
        ps[0, :, cols] = partial(2, cols).astype(BF16)

    tiles(QUARTER // TILE, far)
    for k in order:
        for step in (1, -1):
            rows_k = piece(k, part(step))
            send(("rh", step, k), ps.at[0, rows_k], rh.at[part(step), rows_k], along_s(step))

    for n, j in ((1, 1), (2, -1), (0, 0)):

        def other(cols):
            part_f[n, :, cols] = partial(j, cols)

        tiles(QUARTER // TILE, other)

    for k in order:
        for step in (1, -1):
            mine = piece(k, part(step))
            rest = piece(k, 1 - part(step))
            n = 1 + part(step)
            receive(("rh", step, k), rh.at[part(step), mine])
            ps[n, mine, :] = (part_f[n, mine, :] + rh[part(step), mine, :].astype(F32)).astype(BF16)
            ps[n, rest, :] = part_f[n, rest, :].astype(BF16)
            send(("rf", step, k), ps.at[n, piece(k)], rf.at[part(step), piece(k)], along_s(step))

    for k in order:
        rows_k = piece(k)
        for step in (1, -1):
            receive(("rf", step, k), rf.at[part(step), rows_k])
        total = part_f[0, rows_k, :] + rf[0, rows_k, :].astype(F32) + rf[1, rows_k, :].astype(F32)
        mx[rows_k, :] = total.astype(BF16)
        send(("mx", k), mx.at[rows_k], mixed.at[:, span(fi, QUARTER)], along_f(k, y + 1))

    receive("hid", hid_y)
    receive("gains", gains_y)
    for k in order:
        receive(("mx", k), mixed.at[:, span(lax.rem(fi + 4 - k, 4), QUARTER)])

    m = mixed[...].astype(F32)
    scale2 = lax.rsqrt(jnp.mean(m * m, axis=-1, keepdims=True) + epsilon)
    out_ref[...] = (hid_y[...].astype(F32) + m * scale2 * gains_y[1:2, :]).astype(BF16)

    master_copy.wait()
    for copy in sent:
        copy.wait_send()


def layer(old_master, rows, gains, hidden):
    vmem = pl.BlockSpec(memory_space=pltpu.VMEM)
    anywhere = pl.BlockSpec(memory_space=pl.ANY)
    return pl.pallas_call(
        layer_kernel,
        out_shape=(
            jax.ShapeDtypeStruct((SLAB, D), F32),
            jax.ShapeDtypeStruct((OWN_TOK, D), BF16),
        ),
        in_specs=[anywhere, vmem, vmem, vmem],
        out_specs=(anywhere, vmem),
        scratch_shapes=[
            pltpu.VMEM((SLAB, D), F32),
            pltpu.VMEM((SLAB, D), BF16),
            pltpu.VMEM((256, PIECE), BF16),
            pltpu.VMEM((256, PIECE), BF16),
            pltpu.VMEM((DEVICES, 2 * PIECE), BF16),
            pltpu.VMEM((DEVICES, 2 * PIECE), BF16),
            pltpu.VMEM((SLAB, D), BF16),
            pltpu.VMEM((512, HALF), BF16),
            pltpu.VMEM((OWN_TOK, D), BF16),
            pltpu.VMEM((TOK, HALF), BF16),
            pltpu.VMEM((TOK, 512), F32),
            pltpu.VMEM((TOK, 384), BF16),
            pltpu.VMEM((TOK, 384), BF16),
            pltpu.VMEM((TOK, 384), BF16),
            pltpu.VMEM((2, TOK // 2, 128), BF16),
            pltpu.VMEM((4, TOK // 2, 256), BF16),
            pltpu.VMEM((256, D), BF16),
            pltpu.VMEM((4, 256, QUARTER), BF16),
            pltpu.VMEM((QB, TOK), F32),
            pltpu.VMEM((3, 256, QUARTER), F32),
            pltpu.VMEM((3, 256, QUARTER), BF16),
            pltpu.VMEM((2, 256, QUARTER), BF16),
            pltpu.VMEM((2, 256, QUARTER), BF16),
            pltpu.VMEM((256, QUARTER), BF16),
            pltpu.VMEM((OWN_TOK, D), BF16),
            pltpu.VMEM((OWN_TOK, D), BF16),
            pltpu.VMEM((2, D), F32),
            pltpu.SemaphoreType.DMA((3,)),
            pltpu.SemaphoreType.DMA((16,)),
            pltpu.SemaphoreType.DMA((128,)),
            pltpu.SemaphoreType.DMA((128,)),
        ],
        compiler_params=pltpu.CompilerParams(
            collective_id=0, has_side_effects=True, vmem_limit_bytes=63 * 1024 * 1024
        ),
    )(old_master, rows, gains, hidden)


def body(old_master, old_rows, gains, hidden_in):
    rows = old_rows.reshape(1, SLAB)
    master, hidden_out = layer(old_master, rows, gains[0], hidden_in[0])
    return (master, hidden_out[None])


def solution(mesh):
    in_specs = (
        P(("section", "dp"), None),
        P(("section", "dp")),
        P("section", None, None),
        P("section", "dp", None),
    )
    out_specs = (P(("section", "dp"), None), P("section", "dp", None))
    return jax.shard_map(body, mesh=mesh, in_specs=in_specs, out_specs=out_specs, check_vma=False)
```

time: 166 us -> 147 us (0.89)
  Pallas kernels: 158 us -> 138 us
  local copies, waits for them, and re-layouts: 6.38 us -> 8.55 us
    pallas_call x2 -> x1, Pallas kernels: 158 us -> 138 us  [layer(): pl.pallas_call(layer_kernel, out_shape=(jax.ShapeDtypeStruct((SLAB, D), F...]
    unnamed x7 -> x4, local copies, waits for them, and re-layouts: 5.13 us -> 7.3 us
  transfers between devices with their start and end apart: 1 -> 0, of which waited for: 0 -> 0; matrix products, arithmetic and copies ran while one was open for 0% -> 0% of each run, Pallas kernels for 6% -> 0%
where the time goes in v2:
time: 147 us
  Pallas kernels  138 us (94%)
  local copies, waits for them, and re-layouts  8.55 us (6%)
    pallas_call x1, Pallas kernels, layer(): pl.pallas_call(layer_kernel, out_shape=(jax.ShapeDtypeStruct((SLAB, D), F...  138 us
    unnamed x4, local copies, waits for them, and re-layouts  7.3 us

profile of v2, /device:TPU:0, one launch (start us, length us, event | category | flops | bytes accessed | tf_op | source)
XLA Modules:
  0.0 147.2 jit_solution(13885489625316613074)
XLA Ops:
  0.6 1.2 reshape.7.rows_ref
  1.9 138.0 %shard_map.59 = (f32[384,4608]{1,0:T(8,128)}, bf16[64,4608]{1,0:T(8,128)(2,1)}) custom-call(f32[384,4608]{1,0:T(8,128)} %old_hbm.1, s32[1,384]{1,0:T(1,128)} %reshape.7.rows_ref, f32[2,4608]{1,0:T(2,128)} %bitcast.5, bf16[64,4608]{1,0:T(8,128)(2,1)} %bitcast.4), custom_call_target="tpu_custom_call" | custom-call | tf_op jit(solution)/shard_map/pallas_call | solution.py:523
  139.9 0.0 copy-start
  139.9 6.5 %copy.8 = f32[384,4608]{1,0:T(8,128)} copy(f32[384,4608]{1,0:T(8,128)} %get-tuple-element.8) | data formatting | bytes 14155776
  146.4 0.0 copy-done
  146.4 0.8 copy.9
Async XLA Ops:
  139.9 6.5 %copy-start = (bf16[64,4608]{1,0:T(8,128)(2,1)S(1)}, bf16[64,4608]{1,0:T(8,128)(2,1)}, u32[]{:S(2)}) copy-start(bf16[64,4608]{1,0:T(8,128)(2,1)} %get-tuple-element.5) | copy-start | bytes 1769476

commit v3 on v2

--- a/solution.py
+++ b/solution.py
@@ -167,12 +167,12 @@
 
     own_copy.wait()
     receive("norm", xg.at[other_rows])
-    for colour, step in both:
-        ag_send(colour, "f", step, 0, 0)
-    for colour, step in both:
-        ag_send(colour, "s", step, 0, 0)
-
-    rows = rows_ref[...]
+    for step in (1, -1):
+        ag_send(0, "f", step, 0, 0)
+    for step in (1, -1):
+        ag_send(1, "s", step, 0, 0)
+
+    rows = rows_ref[...].reshape(1, SLAB)
     owner = jnp.floor((rows.astype(F32) + 0.5) * (1.0 / SLAB)).astype(jnp.int32)
     place = rows - owner * SLAB
     dest = iota((DEVICES, SLAB), 0)
@@ -216,23 +216,28 @@
         low = (rest - mid.astype(F32)).astype(BF16)
         old_f[:, cols] = (mm(keep_t, high) + mm(keep_t, mid)) + mm(keep_t, low)
 
-    lax.fori_loop(0, 6, lambda j, t: (keep_rows(span(j, TILE)), t)[1], 0)
-
-    for colour, step in both:
-        ag_recv(colour, "f", step, 0, 0)
-        ag_send(colour, "f", step, -step, 0, part(step))
-        for step2 in (1, -1):
-            ag_send(colour, "s", step2, -step, 0)
-    for colour, step in both:
-        ag_recv(colour, "s", step, 0, 0)
-        ag_send(colour, "s", step, 0, -step, part(step))
-
-    lax.fori_loop(6, D // TILE, lambda j, t: (keep_rows(span(j, TILE)), t)[1], 0)
+    def clear(j, carry):
+        acc[span(j, 64), :] = jnp.zeros((64, 512), F32)
+        return carry
+
+    lax.fori_loop(0, TOK // 64, clear, 0)
+
+    lax.fori_loop(0, 4, lambda j, t: (keep_rows(span(j, TILE)), t)[1], 0)
+
+    for step in (1, -1):
+        ag_recv(0, "f", step, 0, 0)
+        ag_send(0, "f", step, -step, 0, part(step))
 
     own_yz.wait()
     for i, j in across:
         g = lax.rem(y + 4 - i, 4) * 4 + lax.rem(z + 4 - j, 4)
         receive(("yz", i, j), b1.at[span(g, 16)])
+
+    for step in (1, -1):
+        ag_send(1, "f", step, 0, 0)
+    for fk in (0, -1, 1):
+        for step in (1, -1):
+            ag_send(0, "s", step, fk, 0)
 
     r2 = iota((DEVICES, 256), 0)
     from_row = (r2 & 15) * 16 + (r2 >> 4)
@@ -257,19 +262,31 @@
         send(("xc", m), s2.at[span(e, 16)], b3.at[span(e_me, 16)], at(z, lax.div(e, 2), lax.rem(e, 2)))
     own_xc = local(s2.at[span(e_me, 16)], b3.at[span(e_me, 16)])
 
-    for colour in (0, 1):
-        for step in (1, -1):
-            ag_recv(colour, "f", step, -step, 0, part(step))
-        for step in (1, -1):
-            ag_send(colour, "s", step, 2, 0)
-    for fk in (-1, 1):
-        for colour, step in both:
-            ag_recv(colour, "s", step, fk, 0)
-            ag_send(colour, "s", step, fk, -step, part(step))
+    for step in (1, -1):
+        ag_recv(0, "f", step, -step, 0, part(step))
+    for step in (1, -1):
+        ag_send(0, "s", step, 2, 0)
+
+    lax.fori_loop(4, D // TILE, lambda j, t: (keep_rows(span(j, TILE)), t)[1], 0)
+
+    for step in (1, -1):
+        ag_recv(1, "f", step, 0, 0)
+        ag_send(1, "f", step, -step, 0, part(step))
+    for step in (1, -1):
+        ag_recv(1, "s", step, 0, 0)
 
     own_xc.wait()
     for m in (4, 3, 5, 2, 6, 1, 7):
         receive(("xc", m), b3.at[span(lax.rem(e_me + 8 - m, 8), 16)])
+
+    for step in (1, -1):
+        ag_send(1, "s", step, 0, -step, part(step))
+    for fk in (-1, 1):
+        for step in (1, -1):
+            ag_send(1, "s", step, fk, 0)
+    for step in (1, -1):
+        ag_recv(0, "s", step, 0, 0)
+        ag_send(0, "s", step, 0, -step, part(step))
 
     low_lab = b3[:, D : D + 128]
     high_lab = b3[:, D + 128 :]
@@ -302,9 +319,15 @@
         local(w.at[256:384], of.at[o_rows]),
     ]
 
-    for colour, step in both:
-        ag_recv(colour, "s", step, 2, 0)
-        ag_send(colour, "s", step, 2, -step, part(step))
+    for step in (1, -1):
+        ag_recv(1, "f", step, -step, 0, part(step))
+    for step in (1, -1):
+        ag_send(1, "s", step, 2, 0)
+    for fk in (-1, 1):
+        for colour in (0, 1):
+            for step in (1, -1):
+                ag_recv(colour, "s", step, fk, 0)
+                ag_send(colour, "s", step, fk, -step, part(step))
 
     for copy in own_w:
         copy.wait()
@@ -322,11 +345,7 @@
     def along_s(k):
         return at(z + (1 - c) * k, x + c * k, c)
 
-    for k in (2, 1, 3):
-        send(("ow", k), of.at[:, span(lax.rem(fi + k, 4), QUARTER)], ow.at[fi], along_f(k))
-    own_o = local(of.at[:, span(fi, QUARTER)], ow.at[fi])
-
-    def project(colour, fk, fresh):
+    def project(colour, fk):
         if colour == 0:
             xx = lax.rem(x + fk + 4, 4)
             places = [pl.ds(pl.multiple_of((q * 4 + xx) * 128, 128), 128) for q in range(4)]
@@ -338,13 +357,31 @@
         out = mm(block, wp[:, cols], NT_DIMS)
         for q, p in enumerate(places):
             piece = out[q * 128 : (q + 1) * 128]
-            acc[p, :] = piece if fresh else acc[p, :] + piece
-
-    for colour in (0, 1):
-        for fk in (0, -1, 1, 2):
+            acc[p, :] = acc[p, :] + piece
+
+    def tokens_of(fk):
+        for colour in (0, 1):
             for step in (1, -1):
                 ag_recv(colour, "s", step, fk, -step, part(step))
-            project(colour, fk, colour == 0)
+
+    tokens_of(0)
+    project(0, 0)
+    project(1, 0)
+    for colour, step in both:
+        ag_recv(colour, "s", step, 2, 0)
+        ag_send(colour, "s", step, 2, -step, part(step))
+    tokens_of(-1)
+    project(0, -1)
+    project(1, -1)
+    tokens_of(1)
+    project(0, 1)
+    project(1, 1)
+    tokens_of(2)
+    for k in (2, 1, 3):
+        send(("ow", k), of.at[:, span(lax.rem(fi + k, 4), QUARTER)], ow.at[fi], along_f(k))
+    own_o = local(of.at[:, span(fi, QUARTER)], ow.at[fi])
+    project(0, 2)
+    project(1, 2)
 
     for g in range(4):
         at_rows = pl.ds(g * GROUP, GROUP)
@@ -437,29 +474,35 @@
     gather_1(3)
     gather_3(2)
     gather_2(3)
-    gather_3(3)
-    for g in range(4):
+
+    def products(g):
         for step in (1, -1):
             receive(("hg2", step, g), hg.at[f_at(2), rows_g(g, part(step))])
+
+        def columns(cols):
+            out = None
+            for f in range(4):
+                o = mm(hg[f, rows_g(g), :], ow[f, :, cols])
+                out = o if out is None else out + o
+            part_f[rows_g(g), cols] = out
+
+        tiles(QUARTER // TILE, columns)
 
     own_o.wait()
     for k in (1, 3, 2):
         receive(("ow", k), ow.at[lax.rem(fi + 4 - k, 4)])
-
-    def partial(j, cols):
-        sg = lax.rem(si + j + 4, 4)
-        out = None
-        for f in range(4):
-            block = jnp.concatenate(
-                [
-                    hg[f, pl.ds(pl.multiple_of(sg * (256 - 192 * c) + q * (64 + 192 * c), 64), 64), :]
-                    for q in range(4)
-                ],
-                axis=0,
-            )
-            o = mm(block, ow[f, :, cols])
-            out = o if out is None else out + o
-        return out
+    products(0)
+    gather_3(3)
+    products(1)
+    products(2)
+    products(3)
+
+    def source(j, k, half=None):
+        s_there = lax.rem(si + j + 4, 4)
+        first = s_there * (256 - 192 * c) + f_at(k) * (64 + 192 * c)
+        if half is None:
+            return pl.ds(pl.multiple_of(first, 64), 64)
+        return pl.ds(pl.multiple_of(first + half * 32, 32), 32)
 
     order = (2, 1, 3, 0)
 
@@ -469,37 +512,28 @@
             return pl.ds(pl.multiple_of(q * 64, 64), 64)
         return pl.ds(pl.multiple_of(q * 64 + half * 32, 32), 32)
 
-    def far(cols):
-        ps[0, :, cols] = partial(2, cols).astype(BF16)
-
-    tiles(QUARTER // TILE, far)
     for k in order:
+        ps[0, piece(k), :] = part_f[source(2, k), :].astype(BF16)
         for step in (1, -1):
             rows_k = piece(k, part(step))
             send(("rh", step, k), ps.at[0, rows_k], rh.at[part(step), rows_k], along_s(step))
 
-    for n, j in ((1, 1), (2, -1), (0, 0)):
-
-        def other(cols):
-            part_f[n, :, cols] = partial(j, cols)
-
-        tiles(QUARTER // TILE, other)
-
     for k in order:
         for step in (1, -1):
-            mine = piece(k, part(step))
-            rest = piece(k, 1 - part(step))
-            n = 1 + part(step)
-            receive(("rh", step, k), rh.at[part(step), mine])
-            ps[n, mine, :] = (part_f[n, mine, :] + rh[part(step), mine, :].astype(F32)).astype(BF16)
-            ps[n, rest, :] = part_f[n, rest, :].astype(BF16)
-            send(("rf", step, k), ps.at[n, piece(k)], rf.at[part(step), piece(k)], along_s(step))
+            h_in = part(step)
+            mine = piece(k, h_in)
+            rest = piece(k, 1 - h_in)
+            n = 1 + h_in
+            ps[n, rest, :] = part_f[source(step, k, 1 - h_in), :].astype(BF16)
+            receive(("rh", step, k), rh.at[h_in, mine])
+            ps[n, mine, :] = (part_f[source(step, k, h_in), :] + rh[h_in, mine, :].astype(F32)).astype(BF16)
+            send(("rf", step, k), ps.at[n, piece(k)], rf.at[h_in, piece(k)], along_s(step))
 
     for k in order:
         rows_k = piece(k)
         for step in (1, -1):
             receive(("rf", step, k), rf.at[part(step), rows_k])
-        total = part_f[0, rows_k, :] + rf[0, rows_k, :].astype(F32) + rf[1, rows_k, :].astype(F32)
+        total = part_f[source(0, k), :] + rf[0, rows_k, :].astype(F32) + rf[1, rows_k, :].astype(F32)
         mx[rows_k, :] = total.astype(BF16)
         send(("mx", k), mx.at[rows_k], mixed.at[:, span(fi, QUARTER)], along_f(k, y + 1))
 
@@ -548,7 +582,7 @@
             pltpu.VMEM((256, D), BF16),
             pltpu.VMEM((4, 256, QUARTER), BF16),
             pltpu.VMEM((QB, TOK), F32),
-            pltpu.VMEM((3, 256, QUARTER), F32),
+            pltpu.VMEM((TOK // 2, QUARTER), F32),
             pltpu.VMEM((3, 256, QUARTER), BF16),
             pltpu.VMEM((2, 256, QUARTER), BF16),
             pltpu.VMEM((2, 256, QUARTER), BF16),
@@ -568,8 +602,7 @@
 
 
 def body(old_master, old_rows, gains, hidden_in):
-    rows = old_rows.reshape(1, SLAB)
-    master, hidden_out = layer(old_master, rows, gains[0], hidden_in[0])
+    master, hidden_out = layer(old_master, old_rows, gains[0], hidden_in[0])
     return (master, hidden_out[None])
 
 

time: 147 us -> 157 us (1.068)
  Pallas kernels: 138 us -> 149 us
    pallas_call x1, Pallas kernels: 138 us -> 149 us  [layer(): pl.pallas_call(layer_kernel, out_shape=(jax.ShapeDtypeStruct((SLAB, D), F...]
where the time goes in v3:
time: 157 us
  Pallas kernels  149 us (95%)
  local copies, waits for them, and re-layouts  7.3 us (5%)
    pallas_call x1, Pallas kernels, layer(): pl.pallas_call(layer_kernel, out_shape=(jax.ShapeDtypeStruct((SLAB, D), F...  149 us
    unnamed x4, local copies, waits for them, and re-layouts  7.3 us

profile of v3, /device:TPU:0, one launch (start us, length us, event | category | flops | bytes accessed | tf_op | source)
XLA Modules:
  0.0 157.3 jit_solution(16750532884466890697)
XLA Ops:
  0.6 149.3 %shard_map.59 = (f32[384,4608]{1,0:T(8,128)}, bf16[64,4608]{1,0:T(8,128)(2,1)}) custom-call(f32[384,4608]{1,0:T(8,128)} %old_hbm.1, s32[384]{0:T(512)} %rows_ref.1, f32[2,4608]{1,0:T(2,128)} %bitcast.5, bf16[64,4608]{1,0:T(8,128)(2,1)} %bitcast.4), custom_call_target="tpu_custom_call" | custom-call | tf_op jit(solution)/shard_map/pallas_call | solution.py:557
  150.0 0.0 copy-start
  150.0 6.5 %copy.8 = f32[384,4608]{1,0:T(8,128)} copy(f32[384,4608]{1,0:T(8,128)} %get-tuple-element.8) | data formatting | bytes 14155776
  156.5 0.0 copy-done
  156.5 0.8 copy.9
Async XLA Ops:
  150.0 6.5 %copy-start = (bf16[64,4608]{1,0:T(8,128)(2,1)S(1)}, bf16[64,4608]{1,0:T(8,128)(2,1)}, u32[]{:S(2)}) copy-start(bf16[64,4608]{1,0:T(8,128)(2,1)} %get-tuple-element.5) | copy-start | bytes 1769476

commit v4 on v2

--- a/solution.py
+++ b/solution.py
@@ -172,7 +172,7 @@
     for colour, step in both:
         ag_send(colour, "s", step, 0, 0)
 
-    rows = rows_ref[...]
+    rows = rows_ref[...].reshape(1, SLAB)
     owner = jnp.floor((rows.astype(F32) + 0.5) * (1.0 / SLAB)).astype(jnp.int32)
     place = rows - owner * SLAB
     dest = iota((DEVICES, SLAB), 0)
@@ -206,9 +206,6 @@
         send(("yz", i, j), s1.at[span(g, 16)], b1.at[span(group_me, 16)], at(z + j, x, c, y + i))
     own_yz = local(s1.at[span(group_me, 16)], b1.at[span(group_me, 16)])
 
-    send("hid", hid_ref, hid_y, at(z, x, c, y + 1))
-    send("gains", gains_ref, gains_y, at(z, x, c, y + 1))
-
     def keep_rows(cols):
         high = old_b[:, cols]
         rest = old_f[:, cols] - high.astype(F32)
@@ -256,6 +253,9 @@
         e = lax.rem(e_me + m, 8)
         send(("xc", m), s2.at[span(e, 16)], b3.at[span(e_me, 16)], at(z, lax.div(e, 2), lax.rem(e, 2)))
     own_xc = local(s2.at[span(e_me, 16)], b3.at[span(e_me, 16)])
+
+    send("hid", hid_ref, hid_y, at(z, x, c, y + 1))
+    send("gains", gains_ref, gains_y, at(z, x, c, y + 1))
 
     for colour in (0, 1):
         for step in (1, -1):
@@ -384,8 +384,11 @@
         out = (out / total).astype(BF16)
         for i in range(QB // 128):
             ci = qb * (QB // 128) + i
-            att[0, ci * 64 : ci * 64 + 64, :] = out[i * 128 : i * 128 + 64]
-            att[1, ci * 64 : ci * 64 + 64, :] = out[i * 128 + 64 : i * 128 + 128]
+            for core in range(2):
+                for half in range(2):
+                    first = i * 128 + core * 64 + half * 32
+                    at_row = half * 512 + ci * 32
+                    att[core, at_row : at_row + 32, :] = out[first : first + 32]
 
     head_cols = span(c, 128)
     head_cols_p = span(1 - c, 128)
@@ -395,7 +398,7 @@
         return lax.rem(fi + k + 4, 4)
 
     def rows_g(g, half=None):
-        return pl.ds(g * 256, 256) if half is None else pl.ds(g * 256 + half * 128, 128)
+        return pl.ds(g * 512, 512) if half is None else pl.ds(g * 512 + half * 256, 256)
 
     def gather_1(g):
         send(("att", g), att.at[1 - c, rows_g(g)], hg.at[si, rows_g(g), head_cols], partner)
@@ -414,103 +417,101 @@
             ref = hg.at[f_at(-step), rows_g(g, part(step))]
             send(("hg2", step, g), ref, ref, along_f(step))
 
-    combine(0)
-    attend(0)
-    attend(1)
+    for g in range(4):
+        combine(g)
+        attend(2 * g)
+        attend(2 * g + 1)
+
+    def products(g):
+        for step in (1, -1):
+            receive(("hg2", step, g), hg.at[f_at(2), rows_g(g, part(step))])
+
+        def columns(cols):
+            out = None
+            for f in range(4):
+                o = mm(hg[f, rows_g(g), :], ow[f, :, cols])
+                out = o if out is None else out + o
+            part_f[rows_g(g), cols] = out
+
+        tiles(QUARTER // TILE, columns)
+
+    def source(j, q, g):
+        s_there = lax.rem(si + j + 4, 4)
+        block = s_there * (4 - 3 * c) + q * (1 + 3 * c)
+        return pl.ds(pl.multiple_of(g * 512 + block * 32, 32), 32)
+
+    def half_rows(g):
+        return pl.ds(g * 64, 64)
+
+    def all_rows(g):
+        return pl.ds(g * 128, 128)
+
+    def q_rows(g, q):
+        return pl.ds(g * 128 + q * 32, 32)
+
+    def reduce_1(g):
+        for q in range(4):
+            ps[0, q_rows(g, q), :] = part_f[source(2, q, g), :].astype(BF16)
+        for step in (1, -1):
+            src = ps.at[0, pl.ds(g * 128 + part(step) * 64, 64)]
+            send(("rh", step, g), src, rh.at[part(step), half_rows(g)], along_s(step))
+
+    def reduce_2(g):
+        for step in (1, -1):
+            h_in = part(step)
+            n = 1 + h_in
+            for q in range(4):
+                if q // 2 != h_in:
+                    ps[n, q_rows(g, q), :] = part_f[source(step, q, g), :].astype(BF16)
+            receive(("rh", step, g), rh.at[h_in, half_rows(g)])
+            for q in range(4):
+                if q // 2 == h_in:
+                    came = rh[h_in, pl.ds(g * 64 + (q % 2) * 32, 32), :].astype(F32)
+                    ps[n, q_rows(g, q), :] = (part_f[source(step, q, g), :] + came).astype(BF16)
+            send(("rf", step, g), ps.at[n, all_rows(g)], rf.at[h_in, all_rows(g)], along_s(step))
+
+    order = (2, 1, 3, 0)
+
+    def reduce_3(g):
+        for step in (1, -1):
+            receive(("rf", step, g), rf.at[part(step), all_rows(g)])
+        for q in range(4):
+            rows_q = q_rows(g, q)
+            came = rf[0, rows_q, :].astype(F32) + rf[1, rows_q, :].astype(F32)
+            mx[rows_q, :] = (part_f[source(0, q, g), :] + came).astype(BF16)
+        for k in order:
+            src = mx.at[pl.ds(pl.multiple_of(g * 128 + f_at(k) * 32, 32), 32)]
+            send(("mx", k, g), src, mixed.at[pl.ds(g * 32, 32), span(fi, QUARTER)], along_f(k, y + 1))
+
+    def finish(g):
+        at_rows = pl.ds(g * 32, 32)
+        for k in order:
+            receive(("mx", k, g), mixed.at[at_rows, span(lax.rem(fi + 4 - k, 4), QUARTER)])
+        m = mixed[at_rows, :].astype(F32)
+        scale2 = lax.rsqrt(jnp.mean(m * m, axis=-1, keepdims=True) + epsilon)
+        out_ref[at_rows, :] = (hid_y[at_rows, :].astype(F32) + m * scale2 * gains_y[1:2, :]).astype(BF16)
+
     gather_1(0)
-    combine(1)
-    attend(2)
+    gather_1(1)
     gather_2(0)
-    attend(3)
-    gather_1(1)
     gather_3(0)
-    combine(2)
-    attend(4)
     gather_2(1)
-    attend(5)
-    gather_1(2)
-    gather_3(1)
-    combine(3)
-    attend(6)
-    gather_2(2)
-    attend(7)
-    gather_1(3)
-    gather_3(2)
-    gather_2(3)
-    gather_3(3)
-    for g in range(4):
-        for step in (1, -1):
-            receive(("hg2", step, g), hg.at[f_at(2), rows_g(g, part(step))])
-
     own_o.wait()
     for k in (1, 3, 2):
         receive(("ow", k), ow.at[lax.rem(fi + 4 - k, 4)])
-
-    def partial(j, cols):
-        sg = lax.rem(si + j + 4, 4)
-        out = None
-        for f in range(4):
-            block = jnp.concatenate(
-                [
-                    hg[f, pl.ds(pl.multiple_of(sg * (256 - 192 * c) + q * (64 + 192 * c), 64), 64), :]
-                    for q in range(4)
-                ],
-                axis=0,
-            )
-            o = mm(block, ow[f, :, cols])
-            out = o if out is None else out + o
-        return out
-
-    order = (2, 1, 3, 0)
-
-    def piece(k, half=None):
-        q = f_at(k)
-        if half is None:
-            return pl.ds(pl.multiple_of(q * 64, 64), 64)
-        return pl.ds(pl.multiple_of(q * 64 + half * 32, 32), 32)
-
-    def far(cols):
-        ps[0, :, cols] = partial(2, cols).astype(BF16)
-
-    tiles(QUARTER // TILE, far)
-    for k in order:
-        for step in (1, -1):
-            rows_k = piece(k, part(step))
-            send(("rh", step, k), ps.at[0, rows_k], rh.at[part(step), rows_k], along_s(step))
-
-    for n, j in ((1, 1), (2, -1), (0, 0)):
-
-        def other(cols):
-            part_f[n, :, cols] = partial(j, cols)
-
-        tiles(QUARTER // TILE, other)
-
-    for k in order:
-        for step in (1, -1):
-            mine = piece(k, part(step))
-            rest = piece(k, 1 - part(step))
-            n = 1 + part(step)
-            receive(("rh", step, k), rh.at[part(step), mine])
-            ps[n, mine, :] = (part_f[n, mine, :] + rh[part(step), mine, :].astype(F32)).astype(BF16)
-            ps[n, rest, :] = part_f[n, rest, :].astype(BF16)
-            send(("rf", step, k), ps.at[n, piece(k)], rf.at[part(step), piece(k)], along_s(step))
-
-    for k in order:
-        rows_k = piece(k)
-        for step in (1, -1):
-            receive(("rf", step, k), rf.at[part(step), rows_k])
-        total = part_f[0, rows_k, :] + rf[0, rows_k, :].astype(F32) + rf[1, rows_k, :].astype(F32)
-        mx[rows_k, :] = total.astype(BF16)
-        send(("mx", k), mx.at[rows_k], mixed.at[:, span(fi, QUARTER)], along_f(k, y + 1))
-
+    products(0)
+    reduce_1(0)
+    gather_3(1)
+    reduce_2(0)
+    products(1)
+    reduce_1(1)
+    reduce_3(0)
+    reduce_2(1)
+    reduce_3(1)
     receive("hid", hid_y)
     receive("gains", gains_y)
-    for k in order:
-        receive(("mx", k), mixed.at[:, span(lax.rem(fi + 4 - k, 4), QUARTER)])
-
-    m = mixed[...].astype(F32)
-    scale2 = lax.rsqrt(jnp.mean(m * m, axis=-1, keepdims=True) + epsilon)
-    out_ref[...] = (hid_y[...].astype(F32) + m * scale2 * gains_y[1:2, :]).astype(BF16)
+    finish(0)
+    finish(1)
 
     master_copy.wait()
     for copy in sent:
@@ -548,9 +549,9 @@
             pltpu.VMEM((256, D), BF16),
             pltpu.VMEM((4, 256, QUARTER), BF16),
             pltpu.VMEM((QB, TOK), F32),
-            pltpu.VMEM((3, 256, QUARTER), F32),
+            pltpu.VMEM((TOK // 2, QUARTER), F32),
             pltpu.VMEM((3, 256, QUARTER), BF16),
-            pltpu.VMEM((2, 256, QUARTER), BF16),
+            pltpu.VMEM((2, 128, QUARTER), BF16),
             pltpu.VMEM((2, 256, QUARTER), BF16),
             pltpu.VMEM((256, QUARTER), BF16),
             pltpu.VMEM((OWN_TOK, D), BF16),
@@ -568,8 +569,7 @@
 
 
 def body(old_master, old_rows, gains, hidden_in):
-    rows = old_rows.reshape(1, SLAB)
-    master, hidden_out = layer(old_master, rows, gains[0], hidden_in[0])
+    master, hidden_out = layer(old_master, old_rows, gains[0], hidden_in[0])
     return (master, hidden_out[None])
 
 

time: 147 us -> 143 us (0.973)
  Pallas kernels: 138 us -> 134 us
    pallas_call x1, Pallas kernels: 138 us -> 134 us  [layer(): pl.pallas_call(layer_kernel, out_shape=(jax.ShapeDtypeStruct((SLAB, D), F...]
where the time goes in v4:
time: 143 us; the launch traced here: 142 us
  Pallas kernels  134 us (94%)
  local copies, waits for them, and re-layouts  7.3 us (5%)
    pallas_call x1, Pallas kernels, layer(): pl.pallas_call(layer_kernel, out_shape=(jax.ShapeDtypeStruct((SLAB, D), F...  134 us
    unnamed x4, local copies, waits for them, and re-layouts  7.3 us

profile of v4, /device:TPU:0, one launch (start us, length us, event | category | flops | bytes accessed | tf_op | source)
XLA Modules:
  0.0 142.4 jit_solution(11187723360237015233)
XLA Ops:
  0.6 134.5 %shard_map.59 = (f32[384,4608]{1,0:T(8,128)}, bf16[64,4608]{1,0:T(8,128)(2,1)}) custom-call(f32[384,4608]{1,0:T(8,128)} %old_hbm.1, s32[384]{0:T(512)} %rows_ref.1, f32[2,4608]{1,0:T(2,128)} %bitcast.5, bf16[64,4608]{1,0:T(8,128)(2,1)} %bitcast.4), custom_call_target="tpu_custom_call" | custom-call | tf_op jit(solution)/shard_map/pallas_call | solution.py:524
  135.1 0.0 copy-start
  135.1 6.5 %copy.8 = f32[384,4608]{1,0:T(8,128)} copy(f32[384,4608]{1,0:T(8,128)} %get-tuple-element.8) | data formatting | bytes 14155776
  141.6 0.0 copy-done
  141.6 0.8 copy.9
Async XLA Ops:
  135.1 6.5 %copy-start = (bf16[64,4608]{1,0:T(8,128)(2,1)S(1)}, bf16[64,4608]{1,0:T(8,128)(2,1)}, u32[]{:S(2)}) copy-start(bf16[64,4608]{1,0:T(8,128)(2,1)} %get-tuple-element.5) | copy-start | bytes 1769476

commit v5 on v4

--- a/solution.py
+++ b/solution.py
@@ -212,6 +212,12 @@
         mid = rest.astype(BF16)
         low = (rest - mid.astype(F32)).astype(BF16)
         old_f[:, cols] = (mm(keep_t, high) + mm(keep_t, mid)) + mm(keep_t, low)
+
+    def clear(j, carry):
+        acc[span(j, 64), :] = jnp.zeros((64, 512), F32)
+        return carry
+
+    lax.fori_loop(0, TOK // 64, clear, 0)
 
     lax.fori_loop(0, 6, lambda j, t: (keep_rows(span(j, TILE)), t)[1], 0)
 
@@ -326,7 +332,7 @@
         send(("ow", k), of.at[:, span(lax.rem(fi + k, 4), QUARTER)], ow.at[fi], along_f(k))
     own_o = local(of.at[:, span(fi, QUARTER)], ow.at[fi])
 
-    def project(colour, fk, fresh):
+    def project(colour, fk):
         if colour == 0:
             xx = lax.rem(x + fk + 4, 4)
             places = [pl.ds(pl.multiple_of((q * 4 + xx) * 128, 128), 128) for q in range(4)]
@@ -338,13 +344,13 @@
         out = mm(block, wp[:, cols], NT_DIMS)
         for q, p in enumerate(places):
             piece = out[q * 128 : (q + 1) * 128]
-            acc[p, :] = piece if fresh else acc[p, :] + piece
-
-    for colour in (0, 1):
-        for fk in (0, -1, 1, 2):
+            acc[p, :] = acc[p, :] + piece
+
+    for fk in (0, -1, 1, 2):
+        for colour in (0, 1):
             for step in (1, -1):
                 ag_recv(colour, "s", step, fk, -step, part(step))
-            project(colour, fk, colour == 0)
+            project(colour, fk)
 
     for g in range(4):
         at_rows = pl.ds(g * GROUP, GROUP)
@@ -356,7 +362,7 @@
         receive(("proj", g), precv.at[at_rows])
         q = acc[at_rows, 0:128] + precv[at_rows, 0:128].astype(F32)
         kv = acc[at_rows, 256:512] + precv[at_rows, 128:384].astype(F32)
-        z_qkv[at_rows, 0:128] = q.astype(BF16)
+        z_qkv[at_rows, 0:128] = (q * score_scale).astype(BF16)
         z_qkv[at_rows, 128:384] = kv.astype(BF16)
 
     def attend(qb):
@@ -364,7 +370,7 @@
         peak = None
         for kb in range(qb + 1):
             cols = slice(kb * QB, (kb + 1) * QB)
-            s = mm(q, z_qkv[cols, 128:256], NT_DIMS) * score_scale
+            s = mm(q, z_qkv[cols, 128:256], NT_DIMS)
             if kb == qb:
                 s = jnp.where(iota((QB, QB), 0) >= iota((QB, QB), 1), s, -1e30)
             sc[:, cols] = s

time: 143 us -> 141 us (0.986)
    pallas_call x1, Pallas kernels: 134 us -> 133 us  [layer(): pl.pallas_call(layer_kernel, out_shape=(jax.ShapeDtypeStruct((SLAB, D), F...]
where the time goes in v5:
time: 141 us; the launch traced here: 140 us
  Pallas kernels  133 us (94%)
  local copies, waits for them, and re-layouts  7.3 us (5%)
    pallas_call x1, Pallas kernels, layer(): pl.pallas_call(layer_kernel, out_shape=(jax.ShapeDtypeStruct((SLAB, D), F...  133 us
    unnamed x4, local copies, waits for them, and re-layouts  7.3 us

profile of v5, /device:TPU:0, one launch (start us, length us, event | category | flops | bytes accessed | tf_op | source)
XLA Modules:
  0.0 140.5 jit_solution(9125009688978990245)
XLA Ops:
  0.6 132.5 %shard_map.59 = (f32[384,4608]{1,0:T(8,128)}, bf16[64,4608]{1,0:T(8,128)(2,1)}) custom-call(f32[384,4608]{1,0:T(8,128)} %old_hbm.1, s32[384]{0:T(512)} %rows_ref.1, f32[2,4608]{1,0:T(2,128)} %bitcast.5, bf16[64,4608]{1,0:T(8,128)(2,1)} %bitcast.4), custom_call_target="tpu_custom_call" | custom-call | tf_op jit(solution)/shard_map/pallas_call | solution.py:530
  133.2 0.0 copy-start
  133.2 6.5 %copy.8 = f32[384,4608]{1,0:T(8,128)} copy(f32[384,4608]{1,0:T(8,128)} %get-tuple-element.8) | data formatting | bytes 14155776
  139.7 0.0 copy-done
  139.7 0.8 copy.9
Async XLA Ops:
  133.2 6.5 %copy-start = (bf16[64,4608]{1,0:T(8,128)(2,1)S(1)}, bf16[64,4608]{1,0:T(8,128)(2,1)}, u32[]{:S(2)}) copy-start(bf16[64,4608]{1,0:T(8,128)(2,1)} %get-tuple-element.5) | copy-start | bytes 1769476

commit v6 on v5

--- a/solution.py
+++ b/solution.py
@@ -500,8 +500,8 @@
     gather_1(0)
     gather_1(1)
     gather_2(0)
+    gather_2(1)
     gather_3(0)
-    gather_2(1)
     own_o.wait()
     for k in (1, 3, 2):
         receive(("ow", k), ow.at[lax.rem(fi + 4 - k, 4)])

time: 141 us -> 139 us (0.986)
  Pallas kernels: 133 us -> 131 us
    pallas_call x1, Pallas kernels: 133 us -> 131 us  [layer(): pl.pallas_call(layer_kernel, out_shape=(jax.ShapeDtypeStruct((SLAB, D), F...]
where the time goes in v6:
time: 139 us
  Pallas kernels  131 us (94%)
  local copies, waits for them, and re-layouts  7.3 us (5%)
    pallas_call x1, Pallas kernels, layer(): pl.pallas_call(layer_kernel, out_shape=(jax.ShapeDtypeStruct((SLAB, D), F...  131 us
    unnamed x4, local copies, waits for them, and re-layouts  7.3 us

profile of v6, /device:TPU:0, one launch (start us, length us, event | category | flops | bytes accessed | tf_op | source)
XLA Modules:
  0.0 138.6 jit_solution(17005740216126613972)
XLA Ops:
  0.6 130.7 %shard_map.59 = (f32[384,4608]{1,0:T(8,128)}, bf16[64,4608]{1,0:T(8,128)(2,1)}) custom-call(f32[384,4608]{1,0:T(8,128)} %old_hbm.1, s32[384]{0:T(512)} %rows_ref.1, f32[2,4608]{1,0:T(2,128)} %bitcast.5, bf16[64,4608]{1,0:T(8,128)(2,1)} %bitcast.4), custom_call_target="tpu_custom_call" | custom-call | tf_op jit(solution)/shard_map/pallas_call | solution.py:530
  131.3 0.0 copy-start
  131.3 6.5 %copy.8 = f32[384,4608]{1,0:T(8,128)} copy(f32[384,4608]{1,0:T(8,128)} %get-tuple-element.8) | data formatting | bytes 14155776
  137.8 0.0 copy-done
  137.8 0.8 copy.9
Async XLA Ops:
  131.3 6.5 %copy-start = (bf16[64,4608]{1,0:T(8,128)(2,1)S(1)}, bf16[64,4608]{1,0:T(8,128)(2,1)}, u32[]{:S(2)}) copy-start(bf16[64,4608]{1,0:T(8,128)(2,1)} %get-tuple-element.5) | copy-start | bytes 1769476
